TPU v7x, 256 devices: a whole 4x4x8 slice. The times are simulated.
256 devices in a mesh: section: 32 (over z_hi, x, core), rep: 8 (over z_lo, y).
Axes of the slice: x: 4, y: 4, z: 8 (z_hi: 4, z_lo: 2; z = z_hi * 2 + z_lo), core: 2. Of those that a mesh axis runs over, the one named last changes fastest.
Arguments:
- features: bfloat16 [65536, 128], P(('section', 'rep')), may hold values from -6 to 6
- weight: bfloat16 [128, 256], replicated, may hold values from -0.5 to 0.5
- bias: float32 [256], replicated, may hold values from -3 to 3
- tile_vals: bfloat16 [32, 32, 16, 6, 128, 128], P('section', 'rep'), may hold values from -0.15625 to 0.15625
- tile_cols: int32 [32, 32, 16, 6], P('section', 'rep'), may hold values from 0 to 15
- tile_counts: int32 [32, 32, 16], P('section', 'rep'), may hold values from 0 to 6, as said below
Outputs:
- hidden_out: bfloat16 [65536, 256], P(('section', 'rep'))
Inputs may be any that keep to these rules, and one draw needn't show every extreme that they name: `tile_counts`: most tile rows have no live slot for a given source block; each block pair i, j has a tile row with exactly 6 live slots.
All inputs are finite; a program needn't handle non-finite values.
Results may differ from a plain program's by a relative error of at most 0.0047.
Values may be sent and summed in bfloat16 or wider, within the bound.
No kernel may reach another device: no remote copies, remote signals or barrier semaphores. Data moves between devices by JAX's collectives and lax.ppermute only.
A program may use at most 128 MiB of HBM per device.

v0:
```python
import jax
import jax.numpy as jnp
from jax import lax
from jax.sharding import PartitionSpec as P


def broadcast(array, axis, root):
    mine = lax.axis_index(axis) == root
    return lax.psum(jnp.where(mine, array, jnp.zeros_like(array)), axis)


def combine_tiles(block, values, columns, counts):
    tile = values.shape[-1]
    hidden = block.shape[1]
    tiled = block.reshape(block.shape[0] // tile, tile, hidden)
    picked = jnp.take(tiled, columns, axis=0)
    live = jnp.arange(columns.shape[1], dtype=jnp.int32)[None, :] < counts[:, None]
    picked = jnp.where(live[:, :, None, None], picked, jnp.zeros((), picked.dtype))
    return jnp.einsum("tpab,tpbh->tah", values, picked, preferred_element_type=jnp.float32)


def body(features, weight, bias, tile_vals, tile_cols, tile_counts):
    slots = tile_vals.shape[1]
    tile = tile_vals.shape[-1]
    hidden = weight.shape[1]
    replica = lax.axis_index("rep")
    product = jnp.dot(features, weight, preferred_element_type=jnp.float32).astype(jnp.bfloat16)
    source = lax.all_gather(product, "rep", axis=0, tiled=True)
    blocks = []
    for slot_index in range(slots):
        root = replica * slots + slot_index
        blocks.append(broadcast(source, "section", root))
    whole_rows = source.shape[0]
    number = whole_rows // tile
    total = jnp.zeros((number, tile, hidden), jnp.float32)
    for slot_index in range(slots):
        total = total + combine_tiles(
            blocks[slot_index],
            tile_vals[0, slot_index],
            tile_cols[0, slot_index],
            tile_counts[0, slot_index],
        )
    summed = lax.psum_scatter(
        total.reshape(number * tile, hidden), "rep", scatter_dimension=0, tiled=True
    )
    return jnp.maximum(summed + bias, 0.0).astype(jnp.bfloat16)


def solution(mesh):
    placed = (
        P(("section", "rep"), None),
        P(),
        P(),
        P("section", "rep", None, None, None, None),
        P("section", "rep", None, None),
        P("section", "rep", None),
    )
    return jax.shard_map(
        body, mesh=mesh, in_specs=placed, out_specs=P(("section", "rep"), None), check_vma=False
    )
```

profile of v0, /device:TPU:1, one launch (start us, length us, event | category | flops | bytes accessed | tf_op | source)
XLA Modules:
  0.0 449.2 jit_solution(8061194782393311602)
XLA Ops:
  6.5 0.0 copy-start
  6.5 0.0 copy-start.4
  6.5 0.0 copy-start.5
  6.5 0.0 all-gather.2.cloned.1.call-start
  6.5 0.8 copy-done
  7.4 1.7 convolution_convert_fusion
  9.0 0.0 all-gather.2.cloned.1.call-update
  9.1 0.0 all-reduce.3.cloned.1.call-start
  9.1 40.5 %all-gather.2.cloned.1.call-done = bf16[2048,256]{1,0:T(8,128)(2,1)} async-done(((bf16[256,256]{1,0:T(8,128)(2,1)}), bf16[2048,256]{1,0:T(8,128)(2,1)}) %all-gather.2.cloned.1.call-update) | async-done | bytes 1048592 | tf_op jit(solution)/shard_map/all_gather | solution.py:28
  49.7 3.3 broadcast_select_fusion.3
  53.0 0.0 all-reduce.3.cloned.1.call-update
  53.0 0.0 reduce-scatter.2.cloned.1.call-start
  53.1 0.0 copy-done.4
  53.1 0.1 copy.27
  53.2 0.1 reshape.170
  53.3 0.1 copy.26
  53.4 0.1 copy.24
  53.5 0.1 reshape.166
  53.6 0.1 copy.23
  53.7 0.1 copy.30
  53.8 0.1 reshape.174
  53.9 0.1 copy.29
  54.0 0.1 copy.21
  54.0 0.1 reshape.162
  54.1 0.1 copy.20
  54.3 0.0 copy-done.5
  54.3 0.1 iota_compare_fusion.2
  54.4 0.1 iota_compare_fusion.3
  54.5 0.1 iota_compare_fusion
  54.5 305.0 %all-reduce.3.cloned.1.call-done = (bf16[16,128,256]{2,1,0:T(8,128)(2,1)}, bf16[16,128,256]{2,1,0:T(8,128)(2,1)}, bf16[16,128,256]{2,1,0:T(8,128)(2,1)}, bf16[16,128,256]{2,1,0:T(8,128)(2,1)}) async-done(((bf16[16,128,256]{2,1,0:T(8,128)(2,1)}, bf16[16,128,256]{2,1,0:T(8,128)(2,1)}, bf16[16,128,256]{2,1,0:T(8,128)(2,1)}, bf16[16,128,256]{2,1,0:T(8,128)(2,1)}), (bf16[16,128,256]{2,1,0:T(8,128)(2,1)}, ...) | async-done | bytes 4194320 | tf_op jit(solution)/shard_map/psum | solution.py:9
  359.5 0.0 copy-start.3
  359.5 7.3 %gather_fusion.2 = bf16[96,128,256]{2,1,0:T(8,128)(2,1)} fusion(bf16[16,128,256]{2,1,0:T(8,128)(2,1)} %get-tuple-element.7, s32[1024]{0:T(1024)S(1)} %pad_clamp_fusion.1), kind=kCustom, calls=%fused_computation.2.clone | custom fusion | bytes 12583296 | tf_op jit(solution)/shard_map/jit(_take)/gather | solution.py:16
  366.8 0.0 copy-done.3
  366.8 0.0 copy-start.2
  366.8 6.0 %gather_fusion.1 = bf16[96,128,256]{2,1,0:T(8,128)(2,1)} fusion(bf16[16,128,256]{2,1,0:T(8,128)(2,1)S(1)} %copy-done.3, s32[1024]{0:T(1024)S(1)} %pad_clamp_fusion.2), kind=kCustom, calls=%fused_computation.1.clone | custom fusion | bytes 12583296 | tf_op jit(solution)/shard_map/jit(_take)/gather | solution.py:16
  372.8 0.0 copy-done.2
  372.8 0.0 copy-start.1
  372.8 5.9 %gather_fusion.3 = bf16[96,128,256]{2,1,0:T(8,128)(2,1)} fusion(bf16[16,128,256]{2,1,0:T(8,128)(2,1)S(1)} %copy-done.2, s32[1024]{0:T(1024)S(1)} %pad_clamp_fusion), kind=kCustom, calls=%fused_computation.3.clone | custom fusion | bytes 12583296 | tf_op jit(solution)/shard_map/jit(_take)/gather | solution.py:16
  378.7 0.0 copy-done.1
  378.7 0.0 slice-start.4
  378.7 6.0 %gather_fusion = bf16[96,128,256]{2,1,0:T(8,128)(2,1)} fusion(bf16[16,128,256]{2,1,0:T(8,128)(2,1)S(1)} %copy-done.1, s32[1024]{0:T(1024)S(1)} %pad_clamp_fusion.3), kind=kCustom, calls=%fused_computation.clone | custom fusion | bytes 12583296 | tf_op jit(solution)/shard_map/jit(_take)/gather | solution.py:16
  384.7 0.0 slice-start.5
  384.7 0.0 slice-start
  384.7 5.3 %fusion.1 = f32[16,256,128,1]{1,2,3,0:T(8,128)S(1)} fusion(bf16[16,6,128,256]{3,2,1,0:T(8,128)(2,1)} %bitcast.84, pred[16,6]{1,0:T(8,128)(4,1)S(1)} %copy.26, pred[16,6]{1,0:T(8,128)(4,1)S(1)} %get-tuple-element.31, bf16[1,4,16,6,128,128]{5,4,3,2,1,0:T(8,128)(2,1)} %param.11), kind=kOutput, calls=%fused_computation.7 | convolution fusion | flops 811597824 | bytes 11534528 | tf_op jit(solution)/shard_map/tpab,tpbh->tah/dot_general | solution.py:19
  390.0 0.0 slice-done.4
  390.0 0.0 slice-done.5
  390.0 0.0 slice-start.1
  390.1 0.0 slice-start.2
  390.1 3.2 fusion.2
  393.3 0.0 slice-start.3
  393.3 0.0 slice-done
  393.3 0.0 slice-done.1
  393.3 3.3 fusion
  396.6 0.0 slice-done.2
  396.6 0.0 slice-done.3
  396.7 0.0 copy-start.6
  396.7 5.0 %bitcast_add_fusion = f32[16,256,128]{1,2,0:T(8,128)} fusion(f32[16,256,128,1]{1,2,3,0:T(8,128)S(1)} %fusion, f32[16,256,128,1]{1,2,3,0:T(8,128)S(1)} %fusion.1, f32[16,256,128,1]{1,2,3,0:T(8,128)S(1)} %fusion.2, bf16[16,6,128,256]{3,2,1,0:T(8,128)(2,1)S(1)} %bitcast.80, pred[16,6]{1,0:T(8,128)(4,1)S(1)} %copy.20, ...), kind=kOutput, calls=%fused_computation.36 | convolution fusion | flops 813170688 | bytes 17825984 | tf_op jit(solution)/shard_map/tpab,tpbh->tah/dot_general | solution.py:19
  401.7 0.0 reduce-scatter.2.cloned.1.call-update
  401.7 39.4 %reduce-scatter.2.cloned.1.call-done = f32[256,256]{1,0:T(8,128)} async-done(((f32[2048,256]{1,0:T(8,128)}), f32[256,256]{1,0:T(8,128)}) %reduce-scatter.2.cloned.1.call-update) | async-done | bytes 262160 | tf_op jit(solution)/shard_map/reduce_scatter | solution.py:43
  441.1 0.0 copy-done.6
  441.1 1.6 maximum_convert_fusion
  (13 shorter events, 0.1 us)
Async XLA Ops:
  6.5 0.8 copy-start
  6.5 46.5 %copy-start.4 = (s32[1,4,16,6]{2,1,3,0:T(4,128)S(1)}, s32[1,4,16,6]{2,1,3,0:T(4,128)}, u32[]{:S(2)}) copy-start(s32[1,4,16,6]{2,1,3,0:T(4,128)} %param.12) | copy-start | bytes 4612
  6.5 47.7 %copy-start.5 = (s32[1,4,16]{2,1,0:T(4,128)S(1)}, s32[1,4,16]{2,1,0:T(4,128)}, u32[]{:S(2)}) copy-start(s32[1,4,16]{2,1,0:T(4,128)} %param.13) | copy-start | bytes 772
  6.5 43.1 %all-gather.2.cloned.1.call-start = ((), (), s32[]{:S(2)}) async-start(), calls=%async_computation.1 | async-start | bytes 1179648 | tf_op jit(solution)/shard_map/all_gather | solution.py:28
  9.1 350.5 %all-reduce.3.cloned.1.call-start = ((), (), s32[]{:S(2)}) async-start(), calls=%async_computation.3 | async-start | bytes 8388608 | tf_op jit(solution)/shard_map/psum | solution.py:9
  53.0 388.1 %reduce-scatter.2.cloned.1.call-start = ((), (), s32[]{:S(2)}) async-start(), calls=%async_computation.2 | async-start | bytes 2359296 | tf_op jit(solution)/shard_map/reduce_scatter | solution.py:43
  359.5 7.3 %copy-start.3 = (bf16[16,128,256]{2,1,0:T(8,128)(2,1)S(1)}, bf16[16,128,256]{2,1,0:T(8,128)(2,1)}, u32[]{:S(2)}) copy-start(bf16[16,128,256]{2,1,0:T(8,128)(2,1)} %get-tuple-element.8) | copy-start | bytes 3145732
  366.8 6.0 %copy-start.2 = (bf16[16,128,256]{2,1,0:T(8,128)(2,1)S(1)}, bf16[16,128,256]{2,1,0:T(8,128)(2,1)}, u32[]{:S(2)}) copy-start(bf16[16,128,256]{2,1,0:T(8,128)(2,1)} %get-tuple-element.6) | copy-start | bytes 3145732
  372.8 6.0 %copy-start.1 = (bf16[16,128,256]{2,1,0:T(8,128)(2,1)S(1)}, bf16[16,128,256]{2,1,0:T(8,128)(2,1)}, u32[]{:S(2)}) copy-start(bf16[16,128,256]{2,1,0:T(8,128)(2,1)} %get-tuple-element.9) | copy-start | bytes 3145732
  378.7 11.3 %slice-start.4 = ((s8[6291456]{0:T(1024)(128)(4,1)}), s8[2097152]{0:T(1024)(128)(4,1)S(1)}, s32[]{:S(2)}) async-start(s8[6291456]{0:T(1024)(128)(4,1)} %bitcast.81), calls=%async_computation.8 | async-start | bytes 4194304
  384.7 5.3 %slice-start.5 = ((s8[6291456]{0:T(1024)(128)(4,1)}), s8[4194304]{0:T(1024)(128)(4,1)S(1)}, s32[]{:S(2)}) async-start(s8[6291456]{0:T(1024)(128)(4,1)} %bitcast.81), calls=%async_computation.9 | async-start | bytes 8388608
  384.7 8.6 %slice-start = ((s8[6291456]{0:T(1024)(128)(4,1)}), s8[4194304]{0:T(1024)(128)(4,1)S(1)}, s32[]{:S(2)}) async-start(s8[6291456]{0:T(1024)(128)(4,1)} %bitcast.75), calls=%async_computation.4 | async-start | bytes 8388608
  390.0 3.3 slice-start.1
  390.1 6.6 %slice-start.2 = ((s8[6291456]{0:T(1024)(128)(4,1)}), s8[4194304]{0:T(1024)(128)(4,1)S(1)}, s32[]{:S(2)}) async-start(s8[6291456]{0:T(1024)(128)(4,1)} %bitcast.78), calls=%async_computation.6 | async-start | bytes 8388608
  393.3 3.4 slice-start.3
  396.7 44.4 %copy-start.6 = (f32[256]{0:T(256)S(1)}, f32[256]{0:T(256)}, u32[]{:S(2)}) copy-start(f32[256]{0:T(256)} %param.10) | copy-start | bytes 3076
Sparse Core Ops, SparseCore 0:
  9.2 40.4 all-gather.1
  53.1 306.3 all-reduce.2
  401.8 39.2 reduce-scatter.1
where the time goes:
time: 454 us; the launch traced here: 449 us
  waiting for transfers between devices  385 us (85%)
  local copies, waits for them, and re-layouts  27.2 us (6%)
  matrix products  18.5 us (4%)
  between operations  13.4 us (3%)
  other arithmetic  5.21 us (1%)
    psum x1, waiting for transfers between devices, broadcast(): return lax.psum(jnp.where(mine, array, jnp.zeros_like(array)), axis)  305 us
    all_gather x1, waiting for transfers between devices, body(): source = lax.all_gather(product, 'rep', axis=0, tiled=True)  40.5 us
    reduce_scatter x1, waiting for transfers between devices, body(): lax.psum_scatter(total.reshape(number * tile, hidden), 'rep', scatter_dim...  39.4 us
    gather x4, local copies, waits for them, and re-layouts, combine_tiles(): picked = jnp.take(tiled, columns, axis=0)  25.2 us
    dot_general x4, matrix products, combine_tiles(): jnp.einsum('tpab,tpbh->tah', values, picked, preferred_element_type=jnp.f...  16.8 us
  transfers between devices with their start and end apart: 3, of which 3 were waited for; matrix products, arithmetic and copies ran while one was open for 0% of the time, Pallas kernels for 0%

commit v1 on v0

v1 whole, which is shorter than its diff:
```python
import functools

import jax
import jax.numpy as jnp
import numpy as np
from jax import lax
from jax.experimental import pallas as pl
from jax.experimental.pallas import tpu as pltpu
from jax.sharding import PartitionSpec as P

SECTIONS, REPS, CHUNKS = 32, 8, 32
TILE = 128
GROUP = 8


def section_of(z, x, core):
    return z * 8 + x * 2 + core


def landing(block, replica):
    z, x, core = block // 8, block // 2 % 4, block % 2
    half, y = replica // 4, replica % 4
    owner = block // 4
    away = (y - owner % 4) % 4
    beside = (x + 1 if x % 2 else x - 1) % 4
    if half == owner // 4:
        up, moves = {2: (0, 0), 1: (0, 1), 3: (1, 0), 0: (1, 1)}[away]
        if half == 0:
            up = -up
    else:
        up, moves = {2: (1, 0), 1: (1, 1), 3: (2, 0), 0: (2, 1)}[away]
        if half == 0:
            up = {1: -1, 2: 2}[up]
    return section_of((z + up) % 4, beside if moves else x, core), owner


def swaps(axis, step):
    pairs = []
    for s in range(SECTIONS):
        z, x, core = s // 8, s // 2 % 4, s % 2
        at = z if axis == "z" else x
        if (step + core) % 2 == 0:
            to = at ^ 1
        else:
            to = (at + 1) % 4 if at % 2 else (at - 1) % 4
        pairs.append((s, section_of(to, x, core) if axis == "z" else section_of(z, to, core)))
    return pairs


LAND = []
for _b in range(SECTIONS):
    for _r in range(REPS):
        _s, _o = landing(_b, _r)
        LAND.append((_b * REPS + _r, _s * REPS + _o))
CORES = [(s, s ^ 1) for s in range(SECTIONS)]
STEPS = [swaps("z", 0), swaps("z", 1), swaps("x", 0), swaps("x", 1)]


def chunk_slots():
    held = [None] * (SECTIONS * REPS)
    for source, target in LAND:
        held[target] = [source]
    for pairs in STEPS + [CORES]:
        before = [list(h) for h in held]
        for s, t in pairs:
            for r in range(REPS):
                held[t * REPS + r] = before[t * REPS + r] + before[s * REPS + r]
    table = np.zeros((SECTIONS * REPS, CHUNKS), np.int32)
    for device in range(SECTIONS * REPS):
        replica = device % REPS
        for place, chunk in enumerate(held[device]):
            table[device, chunk - replica * CHUNKS] = place
        assert sorted(table[device]) == list(range(CHUNKS))
    return table


SLOTS = chunk_slots()


def list_kernel(per_row, counts, cols, slots, entries, number):
    rows = counts.shape[0]
    trows = rows // 4

    def add(row, done):
        live = counts[row]
        block = row // trows

        def one(p, carry):
            tile = row * per_row + p
            col = cols[tile]
            place = slots[block * 8 + col // 2] * 2 + col % 2
            entries[done + p] = tile + place * 512 + (row % trows) * 65536
            return carry

        lax.fori_loop(0, live, one, 0)
        return done + live

    total = lax.fori_loop(0, rows, add, 0)
    number[0] = (total + GROUP - 1) // GROUP
    for extra in range(GROUP):
        entries[total + extra] = 2 * CHUNKS * 512


def tiles_kernel(entries, number, vals, x0, x1, x2, x3, out, xs, acc):
    rows = x0.shape[0]
    for k, piece in enumerate((x0, x1, x2, x3)):
        xs[k * rows : (k + 1) * rows, :] = piece[...]
    xs[4 * rows :, :] = jnp.zeros((TILE, TILE), xs.dtype)
    acc[...] = jnp.zeros_like(acc)

    def step(g, carry):
        products = []
        for k in range(GROUP):
            entry = entries[g * GROUP + k]
            place = pl.multiple_of((entry // 512 % 128) * TILE, TILE)
            products.append(
                (
                    pl.multiple_of(entry // 65536 * TILE, TILE),
                    jnp.dot(vals[entry % 512], xs[pl.ds(place, TILE), :], preferred_element_type=jnp.float32),
                )
            )
        for at, product in products:
            acc[pl.ds(at, TILE), :] += product
        return carry

    lax.fori_loop(0, number[0], step, 0)
    out[...] = acc[...].astype(out.dtype)


def finish_kernel(parts, weight, bias, out):
    total = parts[0].astype(jnp.float32)
    for k in range(1, REPS):
        total = total + parts[k].astype(jnp.float32)
    high = total.astype(jnp.bfloat16)
    low = (total - high.astype(jnp.float32)).astype(jnp.bfloat16)
    hidden = jnp.dot(high, weight[...], preferred_element_type=jnp.float32)
    hidden = hidden + jnp.dot(low, weight[...], preferred_element_type=jnp.float32)
    out[...] = jnp.maximum(hidden + bias[...], 0.0).astype(out.dtype)


SMEM = pl.BlockSpec(memory_space=pltpu.SMEM)
VMEM = pl.BlockSpec(memory_space=pltpu.VMEM)


def body(features, weight, bias, tile_vals, tile_cols, tile_counts):
    _, blocks, trows, per_row, tile, _ = tile_vals.shape
    tiles = blocks * trows * per_row
    feat = features.shape[1]
    device = lax.axis_index("section") * REPS + lax.axis_index("rep")
    slots = lax.dynamic_slice(jnp.asarray(SLOTS), (device, 0), (1, CHUNKS)).reshape(CHUNKS)

    entries, number = pl.pallas_call(
        functools.partial(list_kernel, per_row),
        out_shape=(
            jax.ShapeDtypeStruct((tiles + GROUP,), jnp.int32),
            jax.ShapeDtypeStruct((1,), jnp.int32),
        ),
        in_specs=[SMEM] * 3,
        out_specs=(SMEM, SMEM),
        cost_estimate=pl.CostEstimate(flops=4000, bytes_accessed=4096, transcendentals=0),
        name="list_live_tiles",
    )(tile_counts.reshape(-1), tile_cols.reshape(-1), slots)

    held = lax.ppermute(features, ("section", "rep"), LAND)
    for pairs in STEPS[:-1]:
        held = jnp.concatenate([held, lax.ppermute(held, "section", pairs)], 0)
    last = lax.ppermute(held, "section", STEPS[-1])
    pieces = (held, last, lax.ppermute(held, "section", CORES), lax.ppermute(last, "section", CORES))

    partial_sums = pl.pallas_call(
        tiles_kernel,
        out_shape=jax.ShapeDtypeStruct((trows * tile, feat), jnp.bfloat16),
        in_specs=[SMEM] * 2 + [VMEM] * 5,
        out_specs=VMEM,
        scratch_shapes=[
            pltpu.VMEM((CHUNKS * features.shape[0] + TILE, feat), jnp.bfloat16),
            pltpu.VMEM((trows * tile, feat), jnp.float32),
        ],
        compiler_params=pltpu.CompilerParams(vmem_limit_bytes=40 * 2**20),
        cost_estimate=pl.CostEstimate(flops=2 * 60 * tile * tile * feat, bytes_accessed=8 * 2**20, transcendentals=0),
        name="sum_live_tiles",
    )(entries, number, tile_vals.reshape(tiles, tile, tile), *pieces)

    parts = lax.all_to_all(partial_sums, "rep", 0, 0, tiled=True)
    own = features.shape[0]
    return pl.pallas_call(
        finish_kernel,
        out_shape=jax.ShapeDtypeStruct((own, weight.shape[1]), jnp.bfloat16),
        in_specs=[VMEM] * 3,
        out_specs=VMEM,
        cost_estimate=pl.CostEstimate(flops=4 * own * feat * weight.shape[1], bytes_accessed=2**20, transcendentals=0),
        name="apply_weight",
    )(parts.reshape(REPS, own, feat), weight, bias.reshape(1, -1))


def solution(mesh):
    placed = (
        P(("section", "rep"), None),
        P(),
        P(),
        P("section", "rep", None, None, None, None),
        P("section", "rep", None, None),
        P("section", "rep", None),
    )
    return jax.shard_map(
        body, mesh=mesh, in_specs=placed, out_specs=P(("section", "rep"), None), check_vma=False
    )
```

time: 454 us -> 76.1 us (0.17)
  waiting for transfers between devices: 385 us -> 11.6 us
  starting transfers between devices: 0.09 us -> 30.7 us
  local copies, waits for them, and re-layouts: 27.2 us -> 4.82 us
  matrix products: 18.5 us -> 0 us
  blocking collectives: 0 us -> 16 us
  between operations: 13.4 us -> 0.08 us
  Pallas kernels: 0 us -> 12 us
  other arithmetic: 5.21 us -> 0.03 us
    psum x1 -> x0, waiting for transfers between devices: 305 us -> none  [broadcast(): return lax.psum(jnp.where(mine, array, jnp.zeros_like(array)), axis)]
    all_gather x1 -> x0, waiting for transfers between devices: 40.5 us -> none  [body(): source = lax.all_gather(product, 'rep', axis=0, tiled=True)]
    reduce_scatter x1 -> x0, waiting for transfers between devices: 39.4 us -> none  [body(): lax.psum_scatter(total.reshape(number * tile, hidden), 'rep', scatter_dim...]
    ppermute x0 -> x7, starting transfers between devices: none -> 30.7 us  [the longest x3 9.98 us: body(): held = jnp.concatenate([held, lax.ppermute(held, 'section', pairs)], 0)]
    gather x4 -> x0, local copies, waits for them, and re-layouts: 25.2 us -> none  [combine_tiles(): picked = jnp.take(tiled, columns, axis=0)]
    dot_general x5 -> x0, matrix products: 18.5 us -> none  [the longest x4 16.8 us: combine_tiles(): jnp.einsum('tpab,tpbh->tah', values, picked, preferred_element_type=jnp.f...]
    all_to_all x0 -> x1, blocking collectives: none -> 16 us  [body(): parts = lax.all_to_all(partial_sums, 'rep', 0, 0, tiled=True)]
    pallas_call x0 -> x3, Pallas kernels: none -> 12 us  [the longest x1 7.01 us: body(): pl.pallas_call(tiles_kernel, out_shape=jax.ShapeDtypeStruct((trows * tile...]
  transfers between devices with their start and end apart: 3 -> 7, of which waited for: 3 -> 5; matrix products, arithmetic and copies ran while one was open for 0% -> 5% of each run, Pallas kernels for 0% -> 4%
where the time goes in v1:
time: 76.1 us; the launch traced here: 75.3 us
  starting transfers between devices  30.7 us (40%)
  blocking collectives  16 us (21%)
  Pallas kernels  12 us (16%)
  waiting for transfers between devices  11.6 us (15%)
  local copies, waits for them, and re-layouts  4.82 us (6%)
    all_to_all x1, blocking collectives, body(): parts = lax.all_to_all(partial_sums, 'rep', 0, 0, tiled=True)  16 us
    ppermute x3, starting transfers between devices, body(): held = jnp.concatenate([held, lax.ppermute(held, 'section', pairs)], 0)  9.98 us
    ppermute x1, starting transfers between devices, body(): held = lax.ppermute(features, ('section', 'rep'), LAND)  9.04 us
    ppermute x3, waiting for transfers between devices, body(): held = jnp.concatenate([held, lax.ppermute(held, 'section', pairs)], 0)  7.77 us
    pallas_call x1, Pallas kernels, body(): pl.pallas_call(tiles_kernel, out_shape=jax.ShapeDtypeStruct((trows * tile...  7.01 us
    ppermute x1, starting transfers between devices, body(): lax.ppermute(held, 'section', CORES)  6.1 us
    ppermute x1, starting transfers between devices, body(): lax.ppermute(last, 'section', CORES)  5.49 us
    pallas_call x1, Pallas kernels, body(): pl.pallas_call(functools.partial(list_kernel, per_row), out_shape=(jax.Sh...  3.05 us
  transfers between devices with their start and end apart: 7, of which 5 were waited for; matrix products, arithmetic and copies ran while one was open for 5% of the time, Pallas kernels for 4%

profile of v1, /device:TPU:1, one launch (start us, length us, event | category | flops | bytes accessed | tf_op | source)
XLA Modules:
  0.0 75.3 jit_solution(357926902792693568)
XLA Ops:
  0.0 9.0 %collective-permute-start = (bf16[256,128]{1,0:T(8,128)(2,1)}, bf16[256,128]{1,0:T(8,128)(2,1)S(1)}, u32[]{:S(2)}, u32[]{:S(2)}) collective-permute-start(bf16[256,128]{1,0:T(8,128)(2,1)} %param.7), channel_id=1, source_target_pairs={{0,240},{1,48},{2,0},{3,192},{4,176},{5,112},{6,64},{7,128},{8,248... | collective-permute-start | bytes 196616 | tf_op jit(solution)/shard_map/ppermute | solution.py:164
  9.0 1.6 %collective-permute-done = bf16[256,128]{1,0:T(8,128)(2,1)S(1)} collective-permute-done((bf16[256,128]{1,0:T(8,128)(2,1)}, bf16[256,128]{1,0:T(8,128)(2,1)S(1)}, u32[]{:S(2)}, u32[]{:S(2)}) %collective-permute-start) | collective-permute-done | bytes 65568 | tf_op jit(solution)/shard_map/ppermute | solution.py:164
  10.7 3.7 %collective-permute-start.1 = (bf16[256,128]{1,0:T(8,128)(2,1)S(1)}, bf16[256,128]{1,0:T(8,128)(2,1)S(1)}, u32[]{:S(2)}, u32[]{:S(2)}) collective-permute-start(bf16[256,128]{1,0:T(8,128)(2,1)S(1)} %collective-permute-done), channel_id=1, source_target_pairs={{0,64},{8,200},{16,80},{24,216},{32,96},{40,232},{48,112},{56,248}... | collective-permute-start | bytes 196616 | tf_op jit(solution)/shard_map/ppermute | solution.py:166
  14.4 1.7 %collective-permute-done.1 = bf16[256,128]{1,0:T(8,128)(2,1)S(1)} collective-permute-done((bf16[256,128]{1,0:T(8,128)(2,1)S(1)}, bf16[256,128]{1,0:T(8,128)(2,1)S(1)}, u32[]{:S(2)}, u32[]{:S(2)}) %collective-permute-start.1) | collective-permute-done | bytes 65568 | tf_op jit(solution)/shard_map/ppermute | solution.py:166
  16.1 2.5 %collective-permute-start.2 = (bf16[512,128]{1,0:T(8,128)(2,1)S(1)}, bf16[512,128]{1,0:T(8,128)(2,1)S(1)}, u32[]{:S(2)}, u32[]{:S(2)}) collective-permute-start(bf16[512,128]{1,0:T(8,128)(2,1)S(1)} %pad_maximum_fusion.1), channel_id=1, source_target_pairs={{0,192},{8,72},{16,208},{24,88},{32,224},{40,104},{48,240},{56,120... | collective-permute-start | bytes 393224 | tf_op jit(solution)/shard_map/ppermute | solution.py:166
  18.7 2.4 %collective-permute-done.2 = bf16[512,128]{1,0:T(8,128)(2,1)S(1)} collective-permute-done((bf16[512,128]{1,0:T(8,128)(2,1)S(1)}, bf16[512,128]{1,0:T(8,128)(2,1)S(1)}, u32[]{:S(2)}, u32[]{:S(2)}) %collective-permute-start.2) | collective-permute-done | bytes 131104 | tf_op jit(solution)/shard_map/ppermute | solution.py:166
  21.0 3.7 %collective-permute-start.3 = (bf16[1024,128]{1,0:T(8,128)(2,1)S(1)}, bf16[1024,128]{1,0:T(8,128)(2,1)S(1)}, u32[]{:S(2)}, u32[]{:S(2)}) collective-permute-start(bf16[1024,128]{1,0:T(8,128)(2,1)S(1)} %pad_maximum_fusion), channel_id=1, source_target_pairs={{0,16},{8,56},{16,0},{24,40},{32,48},{40,24},{48,32},{56,8},{64,80... | collective-permute-start | bytes 786440 | tf_op jit(solution)/shard_map/ppermute | solution.py:166
  24.8 3.7 %collective-permute-done.3 = bf16[1024,128]{1,0:T(8,128)(2,1)S(1)} collective-permute-done((bf16[1024,128]{1,0:T(8,128)(2,1)S(1)}, bf16[1024,128]{1,0:T(8,128)(2,1)S(1)}, u32[]{:S(2)}, u32[]{:S(2)}) %collective-permute-start.3) | collective-permute-done | bytes 262176 | tf_op jit(solution)/shard_map/ppermute | solution.py:166
  28.6 0.1 collective-permute-start.4
  28.7 6.1 %collective-permute-start.5 = (bf16[2048,128]{1,0:T(8,128)(2,1)S(1)}, bf16[2048,128]{1,0:T(8,128)(2,1)S(1)}, u32[]{:S(2)}, u32[]{:S(2)}) collective-permute-start(bf16[2048,128]{1,0:T(8,128)(2,1)S(1)} %constant_dynamic-update-slice_fusion.x0), channel_id=1, source_target_pairs={{0,8},{8,0},{16,24},{24,16},{32,40},{40,32},{48,56},{56,48},{64,72... | collective-permute-start | bytes 1572872 | tf_op jit(solution)/shard_map/ppermute | solution.py:168
  34.8 2.2 %collective-permute-done.4.x1 = bf16[2048,128]{1,0:T(8,128)(2,1)S(1)} collective-permute-done((bf16[2048,128]{1,0:T(8,128)(2,1)S(1)}, bf16[2048,128]{1,0:T(8,128)(2,1)S(1)}, u32[]{:S(2)}, u32[]{:S(2)}) %collective-permute-start.4) | collective-permute-done | bytes 524320 | tf_op jit(solution)/shard_map/ppermute | solution.py:167
  37.0 5.5 %collective-permute-start.6 = (bf16[2048,128]{1,0:T(8,128)(2,1)S(1)}, bf16[2048,128]{1,0:T(8,128)(2,1)S(1)}, u32[]{:S(2)}, u32[]{:S(2)}) collective-permute-start(bf16[2048,128]{1,0:T(8,128)(2,1)S(1)} %collective-permute-done.4.x1), channel_id=1, source_target_pairs={{0,8},{8,0},{16,24},{24,16},{32,40},{40,32},{48,56},{56,48},{64,72... | collective-permute-start | bytes 1572872 | tf_op jit(solution)/shard_map/ppermute | solution.py:168
  42.5 1.3 %reshape.19.counts = s32[64]{0:T(128)} reshape(s32[1,4,16]{2,1,0:T(4,128)} %param.12) | data formatting | bytes 512 | tf_op jit(solution)/shard_map/reshape | solution.py:162
  43.8 0.8 %copy.8 = s32[1,4,16,6]{3,2,1,0:T(8,128)S(1)} copy(s32[1,4,16,6]{2,1,3,0:T(4,128)} %param.11) | data formatting | bytes 3072 | tf_op args[4]
  44.6 1.2 %dynamic-slice_bitcast_fusion.slots = s32[32]{0:T(128)} fusion(s32[256,32]{1,0:T(8,128)} %constant.17.clone, s32[]{:T(128)S(6)} %select_n.3), kind=kLoop, calls=%fused_computation.6 | loop fusion | bytes 260 | tf_op jit(solution)/shard_map/reshape | solution.py:150
  45.8 0.7 reshape.20.cols
  46.5 3.1 %list_live_tiles.1 = (s32[392]{0:T(512)}, s32[1]{0:T(128)}) custom-call(s32[64]{0:T(128)} %reshape.19.counts, s32[384]{0:T(512)} %reshape.20.cols, s32[32]{0:T(128)} %dynamic-slice_bitcast_fusion.slots), custom_call_target="tpu_custom_call" | custom-call | flops 4000 | bytes 4096 | tf_op jit(solution)/shard_map/list_live_tiles/pallas_call | solution.py:152
  49.6 0.0 collective-permute-done.5.x2
  49.6 0.0 collective-permute-done.6.x3
  49.6 0.0 copy-start
  49.6 0.7 copy-done
  50.3 7.0 %sum_live_tiles.1 = bf16[2048,128]{1,0:T(8,128)(2,1)S(1)} custom-call(s32[392]{0:T(512)S(1)} %copy-done, s32[1]{0:T(128)} %get-tuple-element.8.number, bf16[384,128,128]{2,1,0:T(8,128)(2,1)} %bitcast.8, bf16[2048,128]{1,0:T(8,128)(2,1)S(1)} %constant_dynamic-update-slice_fusion.x0, bf16[2048,128]{1,0:T(8,128)(2,1)S(1)} %collective-permute-done.4.x1, ...), custom_call_target="tpu_custom_call" | custom-call | flops 251658240 | bytes 8388608 | tf_op jit(solution)/shard_map/sum_live_tiles/pallas_call | solution.py:170
  57.3 16.0 %all_to_all.9.parts = bf16[8,256,128]{2,1,0:T(8,128)(2,1)} all-to-all(bf16[8,256,128]{2,1,0:T(8,128)(2,1)S(1)} %bitcast.7), channel_id=1, replica_groups=mesh['section'=32,'rep'=8] {'rep'}, dimensions={0} | all-to-all | bytes 1048576 | tf_op jit(solution)/shard_map/all_to_all | solution.py:184
  73.3 2.0 %apply_weight.1 = bf16[256,256]{1,0:T(8,128)(2,1)} custom-call(bf16[8,256,128]{2,1,0:T(8,128)(2,1)} %all_to_all.9.parts, bf16[128,256]{1,0:T(8,128)(2,1)} %weight.1, f32[1,256]{1,0:T(1,128)} %bitcast.9), custom_call_target="tpu_custom_call" | custom-call | flops 33554432 | bytes 1048576 | tf_op jit(solution)/shard_map/apply_weight/pallas_call | solution.py:186
  (6 shorter events, 0.1 us)
Async XLA Ops:
  0.0 10.7 %collective-permute-start = (bf16[256,128]{1,0:T(8,128)(2,1)}, bf16[256,128]{1,0:T(8,128)(2,1)S(1)}, u32[]{:S(2)}, u32[]{:S(2)}) collective-permute-start(bf16[256,128]{1,0:T(8,128)(2,1)} %param.7), channel_id=1, source_target_pairs={{0,240},{1,48},{2,0},{3,192},{4,176},{5,112},{6,64},{7,128},{8,248... | collective-permute-start | bytes 196616 | tf_op jit(solution)/shard_map/ppermute | solution.py:164
  10.7 5.4 %collective-permute-start.1 = (bf16[256,128]{1,0:T(8,128)(2,1)S(1)}, bf16[256,128]{1,0:T(8,128)(2,1)S(1)}, u32[]{:S(2)}, u32[]{:S(2)}) collective-permute-start(bf16[256,128]{1,0:T(8,128)(2,1)S(1)} %collective-permute-done), channel_id=1, source_target_pairs={{0,64},{8,200},{16,80},{24,216},{32,96},{40,232},{48,112},{56,248}... | collective-permute-start | bytes 196616 | tf_op jit(solution)/shard_map/ppermute | solution.py:166
  16.1 4.9 %collective-permute-start.2 = (bf16[512,128]{1,0:T(8,128)(2,1)S(1)}, bf16[512,128]{1,0:T(8,128)(2,1)S(1)}, u32[]{:S(2)}, u32[]{:S(2)}) collective-permute-start(bf16[512,128]{1,0:T(8,128)(2,1)S(1)} %pad_maximum_fusion.1), channel_id=1, source_target_pairs={{0,192},{8,72},{16,208},{24,88},{32,224},{40,104},{48,240},{56,120... | collective-permute-start | bytes 393224 | tf_op jit(solution)/shard_map/ppermute | solution.py:166
  21.0 7.5 %collective-permute-start.3 = (bf16[1024,128]{1,0:T(8,128)(2,1)S(1)}, bf16[1024,128]{1,0:T(8,128)(2,1)S(1)}, u32[]{:S(2)}, u32[]{:S(2)}) collective-permute-start(bf16[1024,128]{1,0:T(8,128)(2,1)S(1)} %pad_maximum_fusion), channel_id=1, source_target_pairs={{0,16},{8,56},{16,0},{24,40},{32,48},{40,24},{48,32},{56,8},{64,80... | collective-permute-start | bytes 786440 | tf_op jit(solution)/shard_map/ppermute | solution.py:166
  28.6 8.4 %collective-permute-start.4 = (bf16[2048,128]{1,0:T(8,128)(2,1)S(1)}, bf16[2048,128]{1,0:T(8,128)(2,1)S(1)}, u32[]{:S(2)}, u32[]{:S(2)}) collective-permute-start(bf16[2048,128]{1,0:T(8,128)(2,1)S(1)} %constant_dynamic-update-slice_fusion.x0), channel_id=1, source_target_pairs={{0,48},{8,24},{16,32},{24,8},{32,16},{40,56},{48,0},{56,40},{64,11... | collective-permute-start | bytes 1572872 | tf_op jit(solution)/shard_map/ppermute | solution.py:167
  28.7 20.9 %collective-permute-start.5 = (bf16[2048,128]{1,0:T(8,128)(2,1)S(1)}, bf16[2048,128]{1,0:T(8,128)(2,1)S(1)}, u32[]{:S(2)}, u32[]{:S(2)}) collective-permute-start(bf16[2048,128]{1,0:T(8,128)(2,1)S(1)} %constant_dynamic-update-slice_fusion.x0), channel_id=1, source_target_pairs={{0,8},{8,0},{16,24},{24,16},{32,40},{40,32},{48,56},{56,48},{64,72... | collective-permute-start | bytes 1572872 | tf_op jit(solution)/shard_map/ppermute | solution.py:168
  37.0 12.6 %collective-permute-start.6 = (bf16[2048,128]{1,0:T(8,128)(2,1)S(1)}, bf16[2048,128]{1,0:T(8,128)(2,1)S(1)}, u32[]{:S(2)}, u32[]{:S(2)}) collective-permute-start(bf16[2048,128]{1,0:T(8,128)(2,1)S(1)} %collective-permute-done.4.x1), channel_id=1, source_target_pairs={{0,8},{8,0},{16,24},{24,16},{32,40},{40,32},{48,56},{56,48},{64,72... | collective-permute-start | bytes 1572872 | tf_op jit(solution)/shard_map/ppermute | solution.py:168
  49.6 0.7 copy-start

commit v2 on v0

v2 whole, which is shorter than its diff:
```python
import functools

import jax
import jax.numpy as jnp
import numpy as np
from jax import lax
from jax.experimental import pallas as pl
from jax.experimental.pallas import tpu as pltpu
from jax.sharding import PartitionSpec as P

SECTIONS, REPS, CHUNKS = 32, 8, 32
TILE = 128
STAGES = (24, 56, 64)
GROUP = 8


def section_of(z, x, core):
    return z * 8 + x * 2 + core


def partner(at, odd):
    return (at + 1 - 2 * (at % 2)) % 4 if not odd else (at - 1 + 2 * (at % 2)) % 4


def landings(block, replica):
    z, x, core = block // 8, block // 2 % 4, block % 2
    owner = block // 4
    away = (replica % 4 - owner % 4) % 4
    beside = (x + 1 if x % 2 else x - 1) % 4
    near = [z, partner(z, core)]
    if replica // 4 != owner // 4:
        near = [p for p in range(4) if p not in near]
    if away % 3 == 0:
        x = beside
    if away % 2:
        near.reverse()
    if away == 3:
        near.reverse()
    if away == 0:
        near.reverse()
    planes = near + [partner(p, 1 - core) for p in near]
    return [section_of(p, x, core) for p in planes], owner


def swaps(step):
    pairs = []
    for s in range(SECTIONS):
        z, x, core = s // 8, s // 2 % 4, s % 2
        pairs.append((s, section_of(z, partner(x, (step + core) % 2), core)))
    return pairs


LANDS = [[], [], [], []]
for _b in range(SECTIONS):
    for _r in range(REPS):
        _places, _o = landings(_b, _r)
        for _pairs, _s in zip(LANDS, _places):
            _pairs.append((_b * REPS + _r, _s * REPS + _o))
CORES = [(s, s ^ 1) for s in range(SECTIONS)]
X_SWAPS = [swaps(0), swaps(1)]


def chunk_slots():
    def swap(held, pairs):
        got = [None] * len(held)
        for s, t in pairs:
            for r in range(REPS):
                got[t * REPS + r] = held[s * REPS + r]
        return got

    def ring(held, pairs):
        first, second = swap(held, pairs[0]), swap(held, pairs[1])
        return [held, first, second, swap(first, pairs[1])]

    def joined(pieces):
        return [sum(p, []) for p in zip(*pieces)]

    held = [[] for _ in range(SECTIONS * REPS)]
    for pairs in LANDS:
        for source, target in pairs:
            held[target].append(source)
    pieces = ring(held, X_SWAPS)
    held = joined(pieces + [swap(p, CORES) for p in pieces])
    table = np.zeros((SECTIONS * REPS, CHUNKS, 2), np.int32)
    for device in range(SECTIONS * REPS):
        replica = device % REPS
        for place, chunk in enumerate(held[device]):
            table[device, chunk - replica * CHUNKS] = 2 * place, 2 * place + 1
        assert sorted(table[device].ravel()) == list(range(2 * CHUNKS))
    return table.reshape(SECTIONS * REPS, 4, 2 * CHUNKS // 4)


SLOTS = chunk_slots()


def prepare_kernel(small, tile_vals, entries, vals, sem):
    _, blocks, trows = small.shape
    per_row = small.shape[0] - 2
    room = blocks * trows * per_row + GROUP

    def row_copy(row):
        part = pl.ds(row * per_row, per_row)
        return pltpu.make_async_copy(tile_vals.at[part], vals.at[part], sem.at[row])

    ends = (jnp.int32(0),) * len(STAGES)
    for row in range(blocks * trows):
        block, trow = row // trows, row % trows
        live = small[1, block, trow]

        def one(p, ends, row=row, block=block, trow=trow):
            place = small[0, block, small[2 + p, block, trow]]
            entry = place * 512 + (p + (row * per_row + trow * 65536))
            for stage, end in enumerate(ends):
                entries[stage * room + end] = entry
            within = [jnp.where(place < limit, 1, 0) for limit in STAGES[:-1]] + [1]
            return tuple(end + w - v for end, w, v in zip(ends, within, [0] + within[:-1]))

        def some(ends, row=row, live=live, one=one):
            row_copy(row).start()
            return lax.fori_loop(0, live, one, ends)

        ends = lax.cond(live > 0, some, lambda ends: ends, ends)
    for stage, end in enumerate(ends):
        spare = entries[stage * room + jnp.maximum(end - 1, 0)] % 512 + 2 * CHUNKS * 512
        for extra in range(GROUP):
            entries[stage * room + end + extra] = spare
        entries[len(STAGES) * room + stage] = (end + GROUP - 1) // GROUP
    for row in range(blocks * trows):
        pl.when(small[1, row // trows, row % trows] > 0)(row_copy(row).wait)


def stage_kernel(stage, entries, vals, *refs):
    last = stage == len(STAGES) - 1
    *pieces, out, xs, total = refs if last else refs + (refs[-2],)
    before = pieces.pop(0) if stage else None
    base = STAGES[stage - 1] if stage else 0
    room = vals.shape[0] + GROUP
    rows = 0
    for piece in pieces:
        xs[rows : rows + piece.shape[0], :] = piece[...]
        rows += piece.shape[0]
    xs[rows:, :] = jnp.zeros((TILE, xs.shape[1]), xs.dtype)
    total[...] = jnp.zeros_like(total) if before is None else before[...]

    def step(g, carry):
        products = []
        for k in range(GROUP):
            entry = entries[stage * room + g * GROUP + k]
            place = jnp.minimum(entry // 512 % 128 - base, rows // TILE)
            products.append(
                (
                    pl.multiple_of(entry // 65536 * TILE, TILE),
                    jnp.dot(
                        vals[entry % 512],
                        xs[pl.ds(pl.multiple_of(place * TILE, TILE), TILE), :],
                        preferred_element_type=jnp.float32,
                    ),
                )
            )
        for at, product in products:
            total[pl.ds(at, TILE), :] += product
        return carry

    lax.fori_loop(0, entries[len(STAGES) * room + stage], step, 0)
    if last:
        out[...] = total[...].astype(out.dtype)


def finish_kernel(parts, weight, bias, out):
    total = parts[0].astype(jnp.float32)
    for k in range(1, REPS):
        total = total + parts[k].astype(jnp.float32)
    high = total.astype(jnp.bfloat16)
    low = (total - high.astype(jnp.float32)).astype(jnp.bfloat16)
    hidden = jnp.dot(high, weight[...], preferred_element_type=jnp.float32)
    hidden = hidden + jnp.dot(low, weight[...], preferred_element_type=jnp.float32)
    out[...] = jnp.maximum(hidden + bias[...], 0.0).astype(out.dtype)


SMEM = pl.BlockSpec(memory_space=pltpu.SMEM)
VMEM = pl.BlockSpec(memory_space=pltpu.VMEM)
HBM = pl.BlockSpec(memory_space=pltpu.HBM)


def estimate(flops, moved):
    return pl.CostEstimate(flops=flops, bytes_accessed=moved, transcendentals=0)


def body(features, weight, bias, tile_vals, tile_cols, tile_counts):
    _, blocks, trows, per_row, tile, _ = tile_vals.shape
    tiles = blocks * trows * per_row
    own, feat = features.shape
    device = lax.axis_index("section") * REPS + lax.axis_index("rep")

    def swap(array, pairs):
        return lax.ppermute(array, "section", pairs)

    small = jnp.concatenate(
        [
            lax.dynamic_slice(jnp.asarray(SLOTS), (device, 0, 0), (1, blocks, trows)),
            tile_counts,
            tile_cols[0].transpose(2, 0, 1),
        ],
        0,
    )
    landed = [lax.ppermute(features, ("section", "rep"), pairs) for pairs in LANDS]
    entries, vals = pl.pallas_call(
        prepare_kernel,
        out_shape=(
            jax.ShapeDtypeStruct((len(STAGES) * (tiles + GROUP + 1),), jnp.int32),
            jax.ShapeDtypeStruct((tiles, tile, tile), tile_vals.dtype),
        ),
        in_specs=[SMEM, HBM],
        out_specs=(SMEM, VMEM),
        scratch_shapes=[
            pltpu.SemaphoreType.DMA((blocks * trows,)),
        ],
        compiler_params=pltpu.CompilerParams(vmem_limit_bytes=40 * 2**20),
        cost_estimate=estimate(4000, 4 * tile_vals.size),
        name="list_live_tiles",
    )(small, tile_vals.reshape(tiles, tile, tile))
    mine = jnp.concatenate(landed, 0)
    mine, entries, vals = lax.optimization_barrier((mine, entries, vals))

    first = swap(mine, X_SWAPS[0])
    second = swap(mine, X_SWAPS[1])
    third = swap(first, X_SWAPS[1])
    beside = [swap(piece, CORES) for piece in (mine, first, second)]
    def add_stage(stage, before, pieces):
        rows = sum(piece.shape[0] for piece in pieces)
        last = stage == len(STAGES) - 1
        ins = ([before] if stage else []) + list(pieces)
        scratch = [pltpu.VMEM((rows + TILE, feat), jnp.bfloat16)]
        if last:
            scratch.append(pltpu.VMEM((trows * tile, feat), jnp.float32))
        return pl.pallas_call(
            functools.partial(stage_kernel, stage),
            out_shape=jax.ShapeDtypeStruct((trows * tile, feat), jnp.bfloat16 if last else jnp.float32),
            in_specs=[SMEM] + [VMEM] * (1 + len(ins)),
            out_specs=VMEM,
            scratch_shapes=scratch,
            compiler_params=pltpu.CompilerParams(vmem_limit_bytes=24 * 2**20),
            cost_estimate=estimate(2 * rows // 6 * tile * feat, 2**20),
            name=f"sum_stage_{stage}",
        )(entries, vals, *ins)

    acc = add_stage(0, None, (mine, first, second))
    third, acc = lax.optimization_barrier((third, acc))
    final = swap(third, CORES)
    acc = add_stage(1, acc, (third, *beside))
    final, acc = lax.optimization_barrier((final, acc))
    partial_sums = add_stage(2, acc, (final,))

    parts = lax.all_to_all(partial_sums, "rep", 0, 0, tiled=True)
    return pl.pallas_call(
        finish_kernel,
        out_shape=jax.ShapeDtypeStruct((own, weight.shape[1]), jnp.bfloat16),
        in_specs=[VMEM] * 3,
        out_specs=VMEM,
        compiler_params=pltpu.CompilerParams(vmem_limit_bytes=8 * 2**20),
        cost_estimate=estimate(4 * own * feat * weight.shape[1], 2**20),
        name="apply_weight",
    )(parts.reshape(REPS, own, feat), weight, bias.reshape(1, -1))


def solution(mesh):
    placed = (
        P(("section", "rep"), None),
        P(),
        P(),
        P("section", "rep", None, None, None, None),
        P("section", "rep", None, None),
        P("section", "rep", None),
    )
    return jax.shard_map(
        body, mesh=mesh, in_specs=placed, out_specs=P(("section", "rep"), None), check_vma=False
    )
```

time: 454 us -> 58.7 us (0.13)
  waiting for transfers between devices: 385 us -> 10.4 us
  local copies, waits for them, and re-layouts: 27.2 us -> 0.69 us
  starting transfers between devices: 0.09 us -> 22.7 us
  matrix products: 18.5 us -> 0 us
  between operations: 13.4 us -> 0.12 us
  blocking collectives: 0 us -> 13.1 us
  Pallas kernels: 0 us -> 10.7 us
    psum x1 -> x0, waiting for transfers between devices: 305 us -> none  [broadcast(): return lax.psum(jnp.where(mine, array, jnp.zeros_like(array)), axis)]
    all_gather x1 -> x0, waiting for transfers between devices: 40.5 us -> none  [body(): source = lax.all_gather(product, 'rep', axis=0, tiled=True)]
    reduce_scatter x1 -> x0, waiting for transfers between devices: 39.4 us -> none  [body(): lax.psum_scatter(total.reshape(number * tile, hidden), 'rep', scatter_dim...]
    gather x4 -> x0, local copies, waits for them, and re-layouts: 25.2 us -> none  [combine_tiles(): picked = jnp.take(tiled, columns, axis=0)]
    ppermute x0 -> x11, starting transfers between devices: none -> 22.7 us  [the longest x4 18.1 us: body(): lax.ppermute(features, ('section', 'rep'), pairs)]
    dot_general x5 -> x0, matrix products: 18.5 us -> none  [the longest x4 16.8 us: combine_tiles(): jnp.einsum('tpab,tpbh->tah', values, picked, preferred_element_type=jnp.f...]
    all_to_all x0 -> x1, blocking collectives: none -> 13.1 us  [body(): parts = lax.all_to_all(partial_sums, 'rep', 0, 0, tiled=True)]
    pallas_call x0 -> x5, Pallas kernels: none -> 10.7 us  [the longest x3 5.14 us: add_stage(): pl.pallas_call(functools.partial(stage_kernel, stage), out_shape=jax.Shap...]
  transfers between devices with their start and end apart: 3 -> 11, of which waited for: 3 -> 2; matrix products, arithmetic and copies ran while one was open for 0% -> 2% of each run, Pallas kernels for 0% -> 15%
where the time goes in v2:
time: 58.7 us; the launch traced here: 58.5 us
  starting transfers between devices  22.7 us (39%)
  blocking collectives  13.1 us (22%)
  Pallas kernels  10.7 us (18%)
  waiting for transfers between devices  10.4 us (18%)
  other arithmetic  0.73 us (1%)
  local copies, waits for them, and re-layouts  0.69 us (1%)
    ppermute x4, starting transfers between devices, body(): lax.ppermute(features, ('section', 'rep'), pairs)  18.1 us
    all_to_all x1, blocking collectives, body(): parts = lax.all_to_all(partial_sums, 'rep', 0, 0, tiled=True)  13.1 us
    ppermute x7, waiting for transfers between devices, swap(): return lax.ppermute(array, 'section', pairs)  10.4 us
    pallas_call x3, Pallas kernels, add_stage(): pl.pallas_call(functools.partial(stage_kernel, stage), out_shape=jax.Shap...  5.14 us
    pallas_call x1, Pallas kernels, body(): pl.pallas_call(prepare_kernel, out_shape=(jax.ShapeDtypeStruct((len(STAGE...  4.71 us
    ppermute x7, starting transfers between devices, swap(): return lax.ppermute(array, 'section', pairs)  4.54 us
  transfers between devices with their start and end apart: 11, of which 2 were waited for; matrix products, arithmetic and copies ran while one was open for 2% of the time, Pallas kernels for 15%

profile of v2, /device:TPU:1, one launch (start us, length us, event | category | flops | bytes accessed | tf_op | source)
XLA Modules:
  0.0 58.5 jit_solution(6629572966908723046)
XLA Ops:
  0.0 3.3 %collective-permute-start.1 = (bf16[256,128]{1,0:T(8,128)(2,1)}, bf16[256,128]{1,0:T(8,128)(2,1)S(1)}, u32[]{:S(2)}, u32[]{:S(2)}) collective-permute-start(bf16[256,128]{1,0:T(8,128)(2,1)} %param.7), channel_id=1, source_target_pairs={{0,48},{1,0},{2,64},{3,112},{4,176},{5,128},{6,192},{7,240},{8,56}... | collective-permute-start | bytes 196616 | tf_op jit(solution)/shard_map/ppermute | solution.py:206
  3.3 8.9 %collective-permute-start = (bf16[256,128]{1,0:T(8,128)(2,1)}, bf16[256,128]{1,0:T(8,128)(2,1)S(1)}, u32[]{:S(2)}, u32[]{:S(2)}) collective-permute-start(bf16[256,128]{1,0:T(8,128)(2,1)} %param.7), channel_id=1, source_target_pairs={{0,112},{1,64},{2,0},{3,48},{4,240},{5,192},{6,128},{7,176},{8,248... | collective-permute-start | bytes 196616 | tf_op jit(solution)/shard_map/ppermute | solution.py:206
  12.2 2.8 %collective-permute-start.3 = (bf16[256,128]{1,0:T(8,128)(2,1)}, bf16[256,128]{1,0:T(8,128)(2,1)S(1)}, u32[]{:S(2)}, u32[]{:S(2)}) collective-permute-start(bf16[256,128]{1,0:T(8,128)(2,1)} %param.7), channel_id=1, source_target_pairs={{0,240},{1,192},{2,128},{3,176},{4,112},{5,64},{6,0},{7,48},{8,120... | collective-permute-start | bytes 196616 | tf_op jit(solution)/shard_map/ppermute | solution.py:206
  15.0 3.2 %collective-permute-start.2 = (bf16[256,128]{1,0:T(8,128)(2,1)}, bf16[256,128]{1,0:T(8,128)(2,1)S(1)}, u32[]{:S(2)}, u32[]{:S(2)}) collective-permute-start(bf16[256,128]{1,0:T(8,128)(2,1)} %param.7), channel_id=1, source_target_pairs={{0,176},{1,128},{2,192},{3,240},{4,48},{5,0},{6,64},{7,112},{8,184... | collective-permute-start | bytes 196616 | tf_op jit(solution)/shard_map/ppermute | solution.py:206
  18.1 0.7 %constant_dynamic-slice_fusion = s32[1,4,16]{2,1,0:T(4,128)S(1)} fusion(s32[256,4,16]{2,1,0:T(4,128)} %constant.17.clone, s32[]{:T(128)S(6)} %select_n.3), kind=kLoop, calls=%fused_computation.2 | loop fusion | bytes 516 | tf_op jit(solution)/shard_map/dynamic_slice | solution.py:200
  18.8 0.7 %pad_add_fusion.small = s32[8,4,16]{2,1,0:T(4,128)S(1)} fusion(s32[6,4,16]{2,1,0:T(4,128)} %bitcast.9, s32[1,4,16]{2,1,0:T(4,128)} %param.12, s32[1,4,16]{2,1,0:T(4,128)S(1)} %constant_dynamic-slice_fusion), kind=kLoop, calls=%fused_computation.1 | loop fusion | flops 1024 | bytes 4096 | tf_op jit(solution)/shard_map/concatenate | solution.py:198
  19.5 4.7 %list_live_tiles.1 = (s32[1179]{0:T(1024)S(1)}, bf16[384,128,128]{2,1,0:T(8,128)(2,1)S(1)}) custom-call(s32[8,4,16]{2,1,0:T(4,128)S(1)} %pad_add_fusion.small, bf16[384,128,128]{2,1,0:T(8,128)(2,1)} %bitcast.8), custom_call_target="tpu_custom_call" | custom-call | flops 4000 | bytes 25165824 | tf_op jit(solution)/shard_map/list_live_tiles/pallas_call | solution.py:207
  24.3 0.0 collective-permute-done.1
  24.3 0.0 collective-permute-done
  24.3 0.0 collective-permute-done.3
  24.3 0.0 collective-permute-done.2
  24.3 0.1 collective-permute-start.4
  24.4 0.1 collective-permute-start.6
  24.5 8.8 %collective-permute-done.4.refs_1_ = bf16[1024,128]{1,0:T(8,128)(2,1)S(1)} collective-permute-done((bf16[1024,128]{1,0:T(8,128)(2,1)S(1)}, bf16[1024,128]{1,0:T(8,128)(2,1)S(1)}, u32[]{:S(2)}, u32[]{:S(2)}) %collective-permute-start.4) | collective-permute-done | bytes 262176 | tf_op jit(solution)/shard_map/ppermute | solution.py:196
  33.3 0.0 collective-permute-start.5
  33.3 1.9 %collective-permute-start.8 = (bf16[1024,128]{1,0:T(8,128)(2,1)S(1)}, bf16[1024,128]{1,0:T(8,128)(2,1)S(1)}, u32[]{:S(2)}, u32[]{:S(2)}) collective-permute-start(bf16[1024,128]{1,0:T(8,128)(2,1)S(1)} %pad_maximum_fusion.refs_0_), channel_id=1, source_target_pairs={{0,8},{8,0},{16,24},{24,16},{32,40},{40,32},{48,56},{56,48},{64,72... | collective-permute-start | bytes 786440 | tf_op jit(solution)/shard_map/ppermute | solution.py:196
  35.2 0.0 collective-permute-done.6.refs_2_
  35.2 0.0 collective-permute-start.10
  35.2 0.5 collective-permute-start.9
  35.7 1.5 %sum_stage_0.1.refs_0_ = f32[2048,128]{1,0:T(8,128)S(1)} custom-call(s32[1179]{0:T(1024)S(1)} %get-tuple-element.16.entries, bf16[384,128,128]{2,1,0:T(8,128)(2,1)S(1)} %get-tuple-element.17.vals, bf16[1024,128]{1,0:T(8,128)(2,1)S(1)} %pad_maximum_fusion.refs_0_, bf16[1024,128]{1,0:T(8,128)(2,1)S(1)} %collective-permute-done.4.refs_1_, ...), custom_call_target="tpu_custom_call" | custom-call | flops 16777216 | bytes 1048576 | tf_op jit(solution)/shard_map/sum_stage_0/pallas_call | solution.py:236
  37.2 0.0 copy-start
  37.3 0.0 copy-start.1
  37.3 1.6 %collective-permute-done.5.refs_1_ = bf16[1024,128]{1,0:T(8,128)(2,1)S(1)} collective-permute-done((bf16[1024,128]{1,0:T(8,128)(2,1)S(1)}, bf16[1024,128]{1,0:T(8,128)(2,1)S(1)}, u32[]{:S(2)}, u32[]{:S(2)}) %collective-permute-start.5) | collective-permute-done | bytes 262176 | tf_op jit(solution)/shard_map/ppermute | solution.py:196
  38.8 2.0 %collective-permute-start.7 = (bf16[1024,128]{1,0:T(8,128)(2,1)S(1)}, bf16[1024,128]{1,0:T(8,128)(2,1)S(1)}, u32[]{:S(2)}, u32[]{:S(2)}) collective-permute-start(bf16[1024,128]{1,0:T(8,128)(2,1)S(1)} %collective-permute-done.5.refs_1_), channel_id=1, source_target_pairs={{0,8},{8,0},{16,24},{24,16},{32,40},{40,32},{48,56},{56,48},{64,72... | collective-permute-start | bytes 786440 | tf_op jit(solution)/shard_map/ppermute | solution.py:196
  40.8 0.0 collective-permute-done.8.refs_2_
  40.8 0.0 collective-permute-done.10.refs_4_
  40.8 0.0 collective-permute-done.9.refs_3_
  40.8 2.3 %sum_stage_1.1.refs_0_ = f32[2048,128]{1,0:T(8,128)S(1)} custom-call(s32[1179]{0:T(1024)S(1)} %get-tuple-element.16.entries, bf16[384,128,128]{2,1,0:T(8,128)(2,1)S(1)} %get-tuple-element.17.vals, f32[2048,128]{1,0:T(8,128)S(1)} %sum_stage_0.1.refs_0_, bf16[1024,128]{1,0:T(8,128)(2,1)S(1)} %collective-permute-done.5.refs_1_, ...), custom_call_target="tpu_custom_call" | custom-call | flops 22364160 | bytes 1048576 | tf_op jit(solution)/shard_map/sum_stage_1/pallas_call | solution.py:236
  43.2 0.0 collective-permute-done.7.refs_1_
  43.2 1.3 %sum_stage_2.1 = bf16[2048,128]{1,0:T(8,128)(2,1)S(1)} custom-call(s32[1179]{0:T(1024)S(1)} %get-tuple-element.16.entries, bf16[384,128,128]{2,1,0:T(8,128)(2,1)S(1)} %get-tuple-element.17.vals, f32[2048,128]{1,0:T(8,128)S(1)} %sum_stage_1.1.refs_0_, bf16[1024,128]{1,0:T(8,128)(2,1)S(1)} %collective-permute-done.7.refs_1_), custom_call_target="tpu_custom_call" | custom-call | flops 5586944 | bytes 1048576 | tf_op jit(solution)/shard_map/sum_stage_2/pallas_call | solution.py:236
  44.5 13.1 %all_to_all.9.parts = bf16[8,256,128]{2,1,0:T(8,128)(2,1)S(1)} all-to-all(bf16[8,256,128]{2,1,0:T(8,128)(2,1)S(1)} %bitcast.6), channel_id=1, replica_groups=mesh['section'=32,'rep'=8] {'rep'}, dimensions={0} | all-to-all | bytes 1048576 | tf_op jit(solution)/shard_map/all_to_all | solution.py:254
  57.6 0.0 copy-done
  57.6 0.0 copy-done.1
  57.6 0.9 %apply_weight.1 = bf16[256,256]{1,0:T(8,128)(2,1)} custom-call(bf16[8,256,128]{2,1,0:T(8,128)(2,1)S(1)} %all_to_all.9.parts, bf16[128,256]{1,0:T(8,128)(2,1)S(1)} %copy-done, f32[1,256]{1,0:T(1,128)S(1)} %bitcast.7), custom_call_target="tpu_custom_call" | custom-call | flops 33554432 | bytes 1048576 | tf_op jit(solution)/shard_map/apply_weight/pallas_call | solution.py:255
  (1 shorter events, 0.0 us)
Async XLA Ops:
  0.0 24.3 %collective-permute-start.1 = (bf16[256,128]{1,0:T(8,128)(2,1)}, bf16[256,128]{1,0:T(8,128)(2,1)S(1)}, u32[]{:S(2)}, u32[]{:S(2)}) collective-permute-start(bf16[256,128]{1,0:T(8,128)(2,1)} %param.7), channel_id=1, source_target_pairs={{0,48},{1,0},{2,64},{3,112},{4,176},{5,128},{6,192},{7,240},{8,56}... | collective-permute-start | bytes 196616 | tf_op jit(solution)/shard_map/ppermute | solution.py:206
  3.3 21.0 %collective-permute-start = (bf16[256,128]{1,0:T(8,128)(2,1)}, bf16[256,128]{1,0:T(8,128)(2,1)S(1)}, u32[]{:S(2)}, u32[]{:S(2)}) collective-permute-start(bf16[256,128]{1,0:T(8,128)(2,1)} %param.7), channel_id=1, source_target_pairs={{0,112},{1,64},{2,0},{3,48},{4,240},{5,192},{6,128},{7,176},{8,248... | collective-permute-start | bytes 196616 | tf_op jit(solution)/shard_map/ppermute | solution.py:206
  12.2 12.1 %collective-permute-start.3 = (bf16[256,128]{1,0:T(8,128)(2,1)}, bf16[256,128]{1,0:T(8,128)(2,1)S(1)}, u32[]{:S(2)}, u32[]{:S(2)}) collective-permute-start(bf16[256,128]{1,0:T(8,128)(2,1)} %param.7), channel_id=1, source_target_pairs={{0,240},{1,192},{2,128},{3,176},{4,112},{5,64},{6,0},{7,48},{8,120... | collective-permute-start | bytes 196616 | tf_op jit(solution)/shard_map/ppermute | solution.py:206
  15.0 9.3 %collective-permute-start.2 = (bf16[256,128]{1,0:T(8,128)(2,1)}, bf16[256,128]{1,0:T(8,128)(2,1)S(1)}, u32[]{:S(2)}, u32[]{:S(2)}) collective-permute-start(bf16[256,128]{1,0:T(8,128)(2,1)} %param.7), channel_id=1, source_target_pairs={{0,176},{1,128},{2,192},{3,240},{4,48},{5,0},{6,64},{7,112},{8,184... | collective-permute-start | bytes 196616 | tf_op jit(solution)/shard_map/ppermute | solution.py:206
  24.3 9.0 %collective-permute-start.4 = (bf16[1024,128]{1,0:T(8,128)(2,1)S(1)}, bf16[1024,128]{1,0:T(8,128)(2,1)S(1)}, u32[]{:S(2)}, u32[]{:S(2)}) collective-permute-start(bf16[1024,128]{1,0:T(8,128)(2,1)S(1)} %pad_maximum_fusion.refs_0_), channel_id=1, source_target_pairs={{0,16},{8,56},{16,0},{24,40},{32,48},{40,24},{48,32},{56,8},{64,80... | collective-permute-start | bytes 786440 | tf_op jit(solution)/shard_map/ppermute | solution.py:196
  24.4 10.8 %collective-permute-start.6 = (bf16[1024,128]{1,0:T(8,128)(2,1)S(1)}, bf16[1024,128]{1,0:T(8,128)(2,1)S(1)}, u32[]{:S(2)}, u32[]{:S(2)}) collective-permute-start(bf16[1024,128]{1,0:T(8,128)(2,1)S(1)} %pad_maximum_fusion.refs_0_), channel_id=1, source_target_pairs={{0,48},{8,24},{16,32},{24,8},{32,16},{40,56},{48,0},{56,40},{64,11... | collective-permute-start | bytes 786440 | tf_op jit(solution)/shard_map/ppermute | solution.py:196
  33.3 5.5 %collective-permute-start.5 = (bf16[1024,128]{1,0:T(8,128)(2,1)S(1)}, bf16[1024,128]{1,0:T(8,128)(2,1)S(1)}, u32[]{:S(2)}, u32[]{:S(2)}) collective-permute-start(bf16[1024,128]{1,0:T(8,128)(2,1)S(1)} %collective-permute-done.4.refs_1_), channel_id=1, source_target_pairs={{0,48},{8,24},{16,32},{24,8},{32,16},{40,56},{48,0},{56,40},{64,11... | collective-permute-start | bytes 786440 | tf_op jit(solution)/shard_map/ppermute | solution.py:196
  33.3 7.5 %collective-permute-start.8 = (bf16[1024,128]{1,0:T(8,128)(2,1)S(1)}, bf16[1024,128]{1,0:T(8,128)(2,1)S(1)}, u32[]{:S(2)}, u32[]{:S(2)}) collective-permute-start(bf16[1024,128]{1,0:T(8,128)(2,1)S(1)} %pad_maximum_fusion.refs_0_), channel_id=1, source_target_pairs={{0,8},{8,0},{16,24},{24,16},{32,40},{40,32},{48,56},{56,48},{64,72... | collective-permute-start | bytes 786440 | tf_op jit(solution)/shard_map/ppermute | solution.py:196
  35.2 5.6 %collective-permute-start.10 = (bf16[1024,128]{1,0:T(8,128)(2,1)S(1)}, bf16[1024,128]{1,0:T(8,128)(2,1)S(1)}, u32[]{:S(2)}, u32[]{:S(2)}) collective-permute-start(bf16[1024,128]{1,0:T(8,128)(2,1)S(1)} %collective-permute-done.6.refs_2_), channel_id=1, source_target_pairs={{0,8},{8,0},{16,24},{24,16},{32,40},{40,32},{48,56},{56,48},{64,72... | collective-permute-start | bytes 786440 | tf_op jit(solution)/shard_map/ppermute | solution.py:196
  35.2 5.6 %collective-permute-start.9 = (bf16[1024,128]{1,0:T(8,128)(2,1)S(1)}, bf16[1024,128]{1,0:T(8,128)(2,1)S(1)}, u32[]{:S(2)}, u32[]{:S(2)}) collective-permute-start(bf16[1024,128]{1,0:T(8,128)(2,1)S(1)} %collective-permute-done.4.refs_1_), channel_id=1, source_target_pairs={{0,8},{8,0},{16,24},{24,16},{32,40},{40,32},{48,56},{56,48},{64,72... | collective-permute-start | bytes 786440 | tf_op jit(solution)/shard_map/ppermute | solution.py:196
  37.2 20.3 %copy-start = (bf16[128,256]{1,0:T(8,128)(2,1)S(1)}, bf16[128,256]{1,0:T(8,128)(2,1)}, u32[]{:S(2)}) copy-start(bf16[128,256]{1,0:T(8,128)(2,1)} %weight.1) | copy-start | bytes 196612
  37.3 20.3 %copy-start.1 = (f32[256]{0:T(256)S(1)}, f32[256]{0:T(256)}, u32[]{:S(2)}) copy-start(f32[256]{0:T(256)} %param.9) | copy-start | bytes 3076
  38.8 4.3 %collective-permute-start.7 = (bf16[1024,128]{1,0:T(8,128)(2,1)S(1)}, bf16[1024,128]{1,0:T(8,128)(2,1)S(1)}, u32[]{:S(2)}, u32[]{:S(2)}) collective-permute-start(bf16[1024,128]{1,0:T(8,128)(2,1)S(1)} %collective-permute-done.5.refs_1_), channel_id=1, source_target_pairs={{0,8},{8,0},{16,24},{24,16},{32,40},{40,32},{48,56},{56,48},{64,72... | collective-permute-start | bytes 786440 | tf_op jit(solution)/shard_map/ppermute | solution.py:196

commit v3 on v2

--- a/solution.py
+++ b/solution.py
@@ -10,7 +10,7 @@
 
 SECTIONS, REPS, CHUNKS = 32, 8, 32
 TILE = 128
-STAGES = (24, 56, 64)
+STAGES = (32, 56, 64)
 GROUP = 8
 
 
@@ -80,7 +80,8 @@
         for source, target in pairs:
             held[target].append(source)
     pieces = ring(held, X_SWAPS)
-    held = joined(pieces + [swap(p, CORES) for p in pieces])
+    beside = [swap(p, CORES) for p in pieces]
+    held = joined(pieces[:3] + beside[:1] + pieces[3:] + beside[1:])
     table = np.zeros((SECTIONS * REPS, CHUNKS, 2), np.int32)
     for device in range(SECTIONS * REPS):
         replica = device % REPS
@@ -93,14 +94,24 @@
 SLOTS = chunk_slots()
 
 
-def prepare_kernel(small, tile_vals, entries, vals, sem):
+def load_kernel(small, tile_vals, vals, sem):
+    _, blocks, trows = small.shape
+    per_row = small.shape[0] - 2
+
+    def row_copy(row):
+        part = pl.ds(row * per_row, per_row)
+        return pltpu.make_async_copy(tile_vals.at[part], vals.at[part], sem.at[row])
+
+    for row in range(blocks * trows):
+        pl.when(small[1, row // trows, row % trows] > 0)(row_copy(row).start)
+    for row in range(blocks * trows):
+        pl.when(small[1, row // trows, row % trows] > 0)(row_copy(row).wait)
+
+
+def list_kernel(small, entries):
     _, blocks, trows = small.shape
     per_row = small.shape[0] - 2
     room = blocks * trows * per_row + GROUP
-
-    def row_copy(row):
-        part = pl.ds(row * per_row, per_row)
-        return pltpu.make_async_copy(tile_vals.at[part], vals.at[part], sem.at[row])
 
     ends = (jnp.int32(0),) * len(STAGES)
     for row in range(blocks * trows):
@@ -115,8 +126,7 @@
             within = [jnp.where(place < limit, 1, 0) for limit in STAGES[:-1]] + [1]
             return tuple(end + w - v for end, w, v in zip(ends, within, [0] + within[:-1]))
 
-        def some(ends, row=row, live=live, one=one):
-            row_copy(row).start()
+        def some(ends, live=live, one=one):
             return lax.fori_loop(0, live, one, ends)
 
         ends = lax.cond(live > 0, some, lambda ends: ends, ends)
@@ -125,9 +135,6 @@
         for extra in range(GROUP):
             entries[stage * room + end + extra] = spare
         entries[len(STAGES) * room + stage] = (end + GROUP - 1) // GROUP
-    for row in range(blocks * trows):
-        pl.when(small[1, row // trows, row % trows] > 0)(row_copy(row).wait)
-
 
 def stage_kernel(stage, entries, vals, *refs):
     last = stage == len(STAGES) - 1
@@ -204,26 +211,33 @@
         0,
     )
     landed = [lax.ppermute(features, ("section", "rep"), pairs) for pairs in LANDS]
-    entries, vals = pl.pallas_call(
-        prepare_kernel,
-        out_shape=(
-            jax.ShapeDtypeStruct((len(STAGES) * (tiles + GROUP + 1),), jnp.int32),
-            jax.ShapeDtypeStruct((tiles, tile, tile), tile_vals.dtype),
-        ),
-        in_specs=[SMEM, HBM],
-        out_specs=(SMEM, VMEM),
-        scratch_shapes=[
-            pltpu.SemaphoreType.DMA((blocks * trows,)),
-        ],
-        compiler_params=pltpu.CompilerParams(vmem_limit_bytes=40 * 2**20),
-        cost_estimate=estimate(4000, 4 * tile_vals.size),
+    entries = pl.pallas_call(
+        list_kernel,
+        out_shape=jax.ShapeDtypeStruct((len(STAGES) * (tiles + GROUP + 1),), jnp.int32),
+        in_specs=[SMEM],
+        out_specs=SMEM,
+        compiler_params=pltpu.CompilerParams(vmem_limit_bytes=8 * 2**20),
+        cost_estimate=estimate(4000, 4096),
         name="list_live_tiles",
-    )(small, tile_vals.reshape(tiles, tile, tile))
+    )(small)
     mine = jnp.concatenate(landed, 0)
-    mine, entries, vals = lax.optimization_barrier((mine, entries, vals))
+    mine, entries, small, vals = lax.optimization_barrier(
+        (mine, entries, small, tile_vals.reshape(tiles, tile, tile))
+    )
 
     first = swap(mine, X_SWAPS[0])
     second = swap(mine, X_SWAPS[1])
+    vals = pl.pallas_call(
+        load_kernel,
+        out_shape=jax.ShapeDtypeStruct(vals.shape, vals.dtype),
+        in_specs=[SMEM, HBM],
+        out_specs=VMEM,
+        scratch_shapes=[pltpu.SemaphoreType.DMA((blocks * trows,))],
+        compiler_params=pltpu.CompilerParams(vmem_limit_bytes=40 * 2**20),
+        cost_estimate=estimate(4000, 4 * vals.size),
+        name="load_live_tiles",
+    )(small, vals)
+    first, vals = lax.optimization_barrier((first, vals))
     third = swap(first, X_SWAPS[1])
     beside = [swap(piece, CORES) for piece in (mine, first, second)]
     def add_stage(stage, before, pieces):
@@ -244,10 +258,10 @@
             name=f"sum_stage_{stage}",
         )(entries, vals, *ins)
 
-    acc = add_stage(0, None, (mine, first, second))
+    acc = add_stage(0, None, (mine, first, second, beside[0]))
     third, acc = lax.optimization_barrier((third, acc))
     final = swap(third, CORES)
-    acc = add_stage(1, acc, (third, *beside))
+    acc = add_stage(1, acc, (third, *beside[1:]))
     final, acc = lax.optimization_barrier((final, acc))
     partial_sums = add_stage(2, acc, (final,))
 

time: 58.7 us -> 58.1 us (0.990)
  waiting for transfers between devices: 10.4 us -> 1.25 us
  starting transfers between devices: 22.7 us -> 29 us
  blocking collectives: 13.1 us -> 15.1 us
    ppermute x7, waiting for transfers between devices: 10.4 us -> 1.24 us  [swap(): return lax.ppermute(array, 'section', pairs)]
    ppermute x7, starting transfers between devices: 4.54 us -> 10.8 us  [swap(): return lax.ppermute(array, 'section', pairs)]
    all_to_all x1, blocking collectives: 13.1 us -> 15.1 us  [body(): parts = lax.all_to_all(partial_sums, 'rep', 0, 0, tiled=True)]
    pallas_call x1 -> x2, Pallas kernels: 4.71 us -> 5.93 us  [the longest x1 3.09 us: body(): pl.pallas_call(load_kernel, out_shape=jax.ShapeDtypeStruct(vals.shape, va...]
    pallas_call x3, Pallas kernels: 5.14 us -> 4.1 us  [add_stage(): pl.pallas_call(functools.partial(stage_kernel, stage), out_shape=jax.Shap...]
  transfers between devices with their start and end apart: 11 -> 11, of which waited for: 2 -> 1; matrix products, arithmetic and copies ran while one was open for 2% -> 2% of each run, Pallas kernels for 15% -> 15%
where the time goes in v3:
time: 58.1 us; the launch traced here: 57.9 us
  starting transfers between devices  29 us (50%)
  blocking collectives  15.1 us (26%)
  Pallas kernels  10.9 us (19%)
  waiting for transfers between devices  1.25 us (2%)
  other arithmetic  0.73 us (1%)
  local copies, waits for them, and re-layouts  0.69 us (1%)
    ppermute x4, starting transfers between devices, body(): lax.ppermute(features, ('section', 'rep'), pairs)  18.1 us
    all_to_all x1, blocking collectives, body(): parts = lax.all_to_all(partial_sums, 'rep', 0, 0, tiled=True)  15.1 us
    ppermute x7, starting transfers between devices, swap(): return lax.ppermute(array, 'section', pairs)  10.8 us
    pallas_call x3, Pallas kernels, add_stage(): pl.pallas_call(functools.partial(stage_kernel, stage), out_shape=jax.Shap...  4.1 us
    pallas_call x1, Pallas kernels, body(): pl.pallas_call(load_kernel, out_shape=jax.ShapeDtypeStruct(vals.shape, va...  3.09 us
    pallas_call x1, Pallas kernels, body(): pl.pallas_call(list_kernel, out_shape=jax.ShapeDtypeStruct((len(STAGES) *...  2.84 us
    ppermute x7, waiting for transfers between devices, swap(): return lax.ppermute(array, 'section', pairs)  1.24 us
  transfers between devices with their start and end apart: 11, of which 1 were waited for; matrix products, arithmetic and copies ran while one was open for 2% of the time, Pallas kernels for 15%

profile of v3, /device:TPU:1, one launch (start us, length us, event | category | flops | bytes accessed | tf_op | source)
XLA Modules:
  0.0 57.9 jit_solution(16053417724555469936)
XLA Ops:
  0.0 3.3 %collective-permute-start.1 = (bf16[256,128]{1,0:T(8,128)(2,1)}, bf16[256,128]{1,0:T(8,128)(2,1)S(1)}, u32[]{:S(2)}, u32[]{:S(2)}) collective-permute-start(bf16[256,128]{1,0:T(8,128)(2,1)} %param.7), channel_id=1, source_target_pairs={{0,48},{1,0},{2,64},{3,112},{4,176},{5,128},{6,192},{7,240},{8,56}... | collective-permute-start | bytes 196616 | tf_op jit(solution)/shard_map/ppermute | solution.py:213
  3.3 8.9 %collective-permute-start = (bf16[256,128]{1,0:T(8,128)(2,1)}, bf16[256,128]{1,0:T(8,128)(2,1)S(1)}, u32[]{:S(2)}, u32[]{:S(2)}) collective-permute-start(bf16[256,128]{1,0:T(8,128)(2,1)} %param.7), channel_id=1, source_target_pairs={{0,112},{1,64},{2,0},{3,48},{4,240},{5,192},{6,128},{7,176},{8,248... | collective-permute-start | bytes 196616 | tf_op jit(solution)/shard_map/ppermute | solution.py:213
  12.2 2.8 %collective-permute-start.3 = (bf16[256,128]{1,0:T(8,128)(2,1)}, bf16[256,128]{1,0:T(8,128)(2,1)S(1)}, u32[]{:S(2)}, u32[]{:S(2)}) collective-permute-start(bf16[256,128]{1,0:T(8,128)(2,1)} %param.7), channel_id=1, source_target_pairs={{0,240},{1,192},{2,128},{3,176},{4,112},{5,64},{6,0},{7,48},{8,120... | collective-permute-start | bytes 196616 | tf_op jit(solution)/shard_map/ppermute | solution.py:213
  15.0 3.2 %collective-permute-start.2 = (bf16[256,128]{1,0:T(8,128)(2,1)}, bf16[256,128]{1,0:T(8,128)(2,1)S(1)}, u32[]{:S(2)}, u32[]{:S(2)}) collective-permute-start(bf16[256,128]{1,0:T(8,128)(2,1)} %param.7), channel_id=1, source_target_pairs={{0,176},{1,128},{2,192},{3,240},{4,48},{5,0},{6,64},{7,112},{8,184... | collective-permute-start | bytes 196616 | tf_op jit(solution)/shard_map/ppermute | solution.py:213
  18.1 0.7 %constant_dynamic-slice_fusion = s32[1,4,16]{2,1,0:T(4,128)S(1)} fusion(s32[256,4,16]{2,1,0:T(4,128)} %constant.17.clone, s32[]{:T(128)S(6)} %select_n.3), kind=kLoop, calls=%fused_computation.2 | loop fusion | bytes 516 | tf_op jit(solution)/shard_map/dynamic_slice | solution.py:207
  18.8 0.7 %pad_add_fusion.small = s32[8,4,16]{2,1,0:T(4,128)S(1)} fusion(s32[6,4,16]{2,1,0:T(4,128)} %bitcast.9, s32[1,4,16]{2,1,0:T(4,128)} %param.12, s32[1,4,16]{2,1,0:T(4,128)S(1)} %constant_dynamic-slice_fusion), kind=kLoop, calls=%fused_computation.1 | loop fusion | flops 1024 | bytes 4096 | tf_op jit(solution)/shard_map/concatenate | solution.py:205
  19.5 2.8 %list_live_tiles.1.entries = s32[1179]{0:T(1024)S(1)} custom-call(s32[8,4,16]{2,1,0:T(4,128)S(1)} %pad_add_fusion.small), custom_call_target="tpu_custom_call" | custom-call | flops 4000 | bytes 4096 | tf_op jit(solution)/shard_map/list_live_tiles/pallas_call | solution.py:214
  22.4 0.0 collective-permute-done.1
  22.4 0.0 collective-permute-done
  22.4 0.0 collective-permute-done.3
  22.4 0.0 collective-permute-done.2
  22.5 0.1 collective-permute-start.4
  22.6 0.1 collective-permute-start.6
  22.7 3.9 %collective-permute-start.7 = (bf16[1024,128]{1,0:T(8,128)(2,1)S(1)}, bf16[1024,128]{1,0:T(8,128)(2,1)S(1)}, u32[]{:S(2)}, u32[]{:S(2)}) collective-permute-start(bf16[1024,128]{1,0:T(8,128)(2,1)S(1)} %pad_maximum_fusion.refs_0_), channel_id=1, source_target_pairs={{0,8},{8,0},{16,24},{24,16},{32,40},{40,32},{48,56},{56,48},{64,72... | collective-permute-start | bytes 786440 | tf_op jit(solution)/shard_map/ppermute | solution.py:203
  26.5 3.1 %load_live_tiles.1.vals = bf16[384,128,128]{2,1,0:T(8,128)(2,1)S(1)} custom-call(s32[8,4,16]{2,1,0:T(4,128)S(1)} %pad_add_fusion.small, bf16[384,128,128]{2,1,0:T(8,128)(2,1)} %bitcast.8), custom_call_target="tpu_custom_call" | custom-call | flops 4000 | bytes 25165824 | tf_op jit(solution)/shard_map/load_live_tiles/pallas_call | solution.py:230
  29.6 1.2 %collective-permute-done.4.refs_1_ = bf16[1024,128]{1,0:T(8,128)(2,1)S(1)} collective-permute-done((bf16[1024,128]{1,0:T(8,128)(2,1)S(1)}, bf16[1024,128]{1,0:T(8,128)(2,1)S(1)}, u32[]{:S(2)}, u32[]{:S(2)}) %collective-permute-start.4) | collective-permute-done | bytes 262176 | tf_op jit(solution)/shard_map/ppermute | solution.py:203
  30.8 0.0 collective-permute-start.5
  30.9 4.0 %collective-permute-start.9 = (bf16[1024,128]{1,0:T(8,128)(2,1)S(1)}, bf16[1024,128]{1,0:T(8,128)(2,1)S(1)}, u32[]{:S(2)}, u32[]{:S(2)}) collective-permute-start(bf16[1024,128]{1,0:T(8,128)(2,1)S(1)} %collective-permute-done.4.refs_1_), channel_id=1, source_target_pairs={{0,8},{8,0},{16,24},{24,16},{32,40},{40,32},{48,56},{56,48},{64,72... | collective-permute-start | bytes 786440 | tf_op jit(solution)/shard_map/ppermute | solution.py:203
  34.9 0.0 collective-permute-done.6.refs_2_
  34.9 0.0 collective-permute-start.10
  34.9 0.0 collective-permute-done.7.refs_3_
  34.9 1.5 %sum_stage_0.1.refs_0_ = f32[2048,128]{1,0:T(8,128)S(1)} custom-call(s32[1179]{0:T(1024)S(1)} %list_live_tiles.1.entries, bf16[384,128,128]{2,1,0:T(8,128)(2,1)S(1)} %load_live_tiles.1.vals, bf16[1024,128]{1,0:T(8,128)(2,1)S(1)} %pad_maximum_fusion.refs_0_, bf16[1024,128]{1,0:T(8,128)(2,1)S(1)} %collective-permute-done.4.refs_1_, ...), custom_call_target="tpu_custom_call" | custom-call | flops 22364160 | bytes 1048576 | tf_op jit(solution)/shard_map/sum_stage_0/pallas_call | solution.py:250
  36.5 0.0 copy-start
  36.5 0.0 copy-start.1
  36.5 0.0 collective-permute-done.5.refs_1_
  36.5 2.7 %collective-permute-start.8 = (bf16[1024,128]{1,0:T(8,128)(2,1)S(1)}, bf16[1024,128]{1,0:T(8,128)(2,1)S(1)}, u32[]{:S(2)}, u32[]{:S(2)}) collective-permute-start(bf16[1024,128]{1,0:T(8,128)(2,1)S(1)} %collective-permute-done.5.refs_1_), channel_id=1, source_target_pairs={{0,8},{8,0},{16,24},{24,16},{32,40},{40,32},{48,56},{56,48},{64,72... | collective-permute-start | bytes 786440 | tf_op jit(solution)/shard_map/ppermute | solution.py:203
  39.2 0.0 collective-permute-done.10.refs_3_
  39.2 0.0 collective-permute-done.9.refs_2_
  39.2 1.3 %sum_stage_1.1.refs_0_ = f32[2048,128]{1,0:T(8,128)S(1)} custom-call(s32[1179]{0:T(1024)S(1)} %list_live_tiles.1.entries, bf16[384,128,128]{2,1,0:T(8,128)(2,1)S(1)} %load_live_tiles.1.vals, f32[2048,128]{1,0:T(8,128)S(1)} %sum_stage_0.1.refs_0_, bf16[1024,128]{1,0:T(8,128)(2,1)S(1)} %collective-permute-done.5.refs_1_, ...), custom_call_target="tpu_custom_call" | custom-call | flops 16777216 | bytes 1048576 | tf_op jit(solution)/shard_map/sum_stage_1/pallas_call | solution.py:250
  40.5 0.0 collective-permute-done.8.refs_1_
  40.5 1.3 %sum_stage_2.1 = bf16[2048,128]{1,0:T(8,128)(2,1)S(1)} custom-call(s32[1179]{0:T(1024)S(1)} %list_live_tiles.1.entries, bf16[384,128,128]{2,1,0:T(8,128)(2,1)S(1)} %load_live_tiles.1.vals, f32[2048,128]{1,0:T(8,128)S(1)} %sum_stage_1.1.refs_0_, bf16[1024,128]{1,0:T(8,128)(2,1)S(1)} %collective-permute-done.8.refs_1_), custom_call_target="tpu_custom_call" | custom-call | flops 5586944 | bytes 1048576 | tf_op jit(solution)/shard_map/sum_stage_2/pallas_call | solution.py:250
  41.8 15.1 %all_to_all.9.parts = bf16[8,256,128]{2,1,0:T(8,128)(2,1)S(1)} all-to-all(bf16[8,256,128]{2,1,0:T(8,128)(2,1)S(1)} %bitcast.6), channel_id=1, replica_groups=mesh['section'=32,'rep'=8] {'rep'}, dimensions={0} | all-to-all | bytes 1048576 | tf_op jit(solution)/shard_map/all_to_all | solution.py:268
  57.0 0.0 copy-done
  57.0 0.0 copy-done.1
  57.0 0.9 %apply_weight.1 = bf16[256,256]{1,0:T(8,128)(2,1)} custom-call(bf16[8,256,128]{2,1,0:T(8,128)(2,1)S(1)} %all_to_all.9.parts, bf16[128,256]{1,0:T(8,128)(2,1)S(1)} %copy-done, f32[1,256]{1,0:T(1,128)S(1)} %bitcast.7), custom_call_target="tpu_custom_call" | custom-call | flops 33554432 | bytes 1048576 | tf_op jit(solution)/shard_map/apply_weight/pallas_call | solution.py:269
  (1 shorter events, 0.0 us)
Async XLA Ops:
  0.0 22.4 %collective-permute-start.1 = (bf16[256,128]{1,0:T(8,128)(2,1)}, bf16[256,128]{1,0:T(8,128)(2,1)S(1)}, u32[]{:S(2)}, u32[]{:S(2)}) collective-permute-start(bf16[256,128]{1,0:T(8,128)(2,1)} %param.7), channel_id=1, source_target_pairs={{0,48},{1,0},{2,64},{3,112},{4,176},{5,128},{6,192},{7,240},{8,56}... | collective-permute-start | bytes 196616 | tf_op jit(solution)/shard_map/ppermute | solution.py:213
  3.3 19.1 %collective-permute-start = (bf16[256,128]{1,0:T(8,128)(2,1)}, bf16[256,128]{1,0:T(8,128)(2,1)S(1)}, u32[]{:S(2)}, u32[]{:S(2)}) collective-permute-start(bf16[256,128]{1,0:T(8,128)(2,1)} %param.7), channel_id=1, source_target_pairs={{0,112},{1,64},{2,0},{3,48},{4,240},{5,192},{6,128},{7,176},{8,248... | collective-permute-start | bytes 196616 | tf_op jit(solution)/shard_map/ppermute | solution.py:213
  12.2 10.2 %collective-permute-start.3 = (bf16[256,128]{1,0:T(8,128)(2,1)}, bf16[256,128]{1,0:T(8,128)(2,1)S(1)}, u32[]{:S(2)}, u32[]{:S(2)}) collective-permute-start(bf16[256,128]{1,0:T(8,128)(2,1)} %param.7), channel_id=1, source_target_pairs={{0,240},{1,192},{2,128},{3,176},{4,112},{5,64},{6,0},{7,48},{8,120... | collective-permute-start | bytes 196616 | tf_op jit(solution)/shard_map/ppermute | solution.py:213
  15.0 7.4 %collective-permute-start.2 = (bf16[256,128]{1,0:T(8,128)(2,1)}, bf16[256,128]{1,0:T(8,128)(2,1)S(1)}, u32[]{:S(2)}, u32[]{:S(2)}) collective-permute-start(bf16[256,128]{1,0:T(8,128)(2,1)} %param.7), channel_id=1, source_target_pairs={{0,176},{1,128},{2,192},{3,240},{4,48},{5,0},{6,64},{7,112},{8,184... | collective-permute-start | bytes 196616 | tf_op jit(solution)/shard_map/ppermute | solution.py:213
  22.5 8.4 %collective-permute-start.4 = (bf16[1024,128]{1,0:T(8,128)(2,1)S(1)}, bf16[1024,128]{1,0:T(8,128)(2,1)S(1)}, u32[]{:S(2)}, u32[]{:S(2)}) collective-permute-start(bf16[1024,128]{1,0:T(8,128)(2,1)S(1)} %pad_maximum_fusion.refs_0_), channel_id=1, source_target_pairs={{0,16},{8,56},{16,0},{24,40},{32,48},{40,24},{48,32},{56,8},{64,80... | collective-permute-start | bytes 786440 | tf_op jit(solution)/shard_map/ppermute | solution.py:203
  22.6 12.3 %collective-permute-start.6 = (bf16[1024,128]{1,0:T(8,128)(2,1)S(1)}, bf16[1024,128]{1,0:T(8,128)(2,1)S(1)}, u32[]{:S(2)}, u32[]{:S(2)}) collective-permute-start(bf16[1024,128]{1,0:T(8,128)(2,1)S(1)} %pad_maximum_fusion.refs_0_), channel_id=1, source_target_pairs={{0,48},{8,24},{16,32},{24,8},{32,16},{40,56},{48,0},{56,40},{64,11... | collective-permute-start | bytes 786440 | tf_op jit(solution)/shard_map/ppermute | solution.py:203
  22.7 12.2 %collective-permute-start.7 = (bf16[1024,128]{1,0:T(8,128)(2,1)S(1)}, bf16[1024,128]{1,0:T(8,128)(2,1)S(1)}, u32[]{:S(2)}, u32[]{:S(2)}) collective-permute-start(bf16[1024,128]{1,0:T(8,128)(2,1)S(1)} %pad_maximum_fusion.refs_0_), channel_id=1, source_target_pairs={{0,8},{8,0},{16,24},{24,16},{32,40},{40,32},{48,56},{56,48},{64,72... | collective-permute-start | bytes 786440 | tf_op jit(solution)/shard_map/ppermute | solution.py:203
  30.8 5.6 %collective-permute-start.5 = (bf16[1024,128]{1,0:T(8,128)(2,1)S(1)}, bf16[1024,128]{1,0:T(8,128)(2,1)S(1)}, u32[]{:S(2)}, u32[]{:S(2)}) collective-permute-start(bf16[1024,128]{1,0:T(8,128)(2,1)S(1)} %collective-permute-done.4.refs_1_), channel_id=1, source_target_pairs={{0,48},{8,24},{16,32},{24,8},{32,16},{40,56},{48,0},{56,40},{64,11... | collective-permute-start | bytes 786440 | tf_op jit(solution)/shard_map/ppermute | solution.py:203
  30.9 8.4 %collective-permute-start.9 = (bf16[1024,128]{1,0:T(8,128)(2,1)S(1)}, bf16[1024,128]{1,0:T(8,128)(2,1)S(1)}, u32[]{:S(2)}, u32[]{:S(2)}) collective-permute-start(bf16[1024,128]{1,0:T(8,128)(2,1)S(1)} %collective-permute-done.4.refs_1_), channel_id=1, source_target_pairs={{0,8},{8,0},{16,24},{24,16},{32,40},{40,32},{48,56},{56,48},{64,72... | collective-permute-start | bytes 786440 | tf_op jit(solution)/shard_map/ppermute | solution.py:203
  34.9 4.3 %collective-permute-start.10 = (bf16[1024,128]{1,0:T(8,128)(2,1)S(1)}, bf16[1024,128]{1,0:T(8,128)(2,1)S(1)}, u32[]{:S(2)}, u32[]{:S(2)}) collective-permute-start(bf16[1024,128]{1,0:T(8,128)(2,1)S(1)} %collective-permute-done.6.refs_2_), channel_id=1, source_target_pairs={{0,8},{8,0},{16,24},{24,16},{32,40},{40,32},{48,56},{56,48},{64,72... | collective-permute-start | bytes 786440 | tf_op jit(solution)/shard_map/ppermute | solution.py:203
  36.5 20.5 %copy-start = (bf16[128,256]{1,0:T(8,128)(2,1)S(1)}, bf16[128,256]{1,0:T(8,128)(2,1)}, u32[]{:S(2)}) copy-start(bf16[128,256]{1,0:T(8,128)(2,1)} %weight.1) | copy-start | bytes 196612
  36.5 20.5 %copy-start.1 = (f32[256]{0:T(256)S(1)}, f32[256]{0:T(256)}, u32[]{:S(2)}) copy-start(f32[256]{0:T(256)} %param.9) | copy-start | bytes 3076
  36.5 4.0 %collective-permute-start.8 = (bf16[1024,128]{1,0:T(8,128)(2,1)S(1)}, bf16[1024,128]{1,0:T(8,128)(2,1)S(1)}, u32[]{:S(2)}, u32[]{:S(2)}) collective-permute-start(bf16[1024,128]{1,0:T(8,128)(2,1)S(1)} %collective-permute-done.5.refs_1_), channel_id=1, source_target_pairs={{0,8},{8,0},{16,24},{24,16},{32,40},{40,32},{48,56},{56,48},{64,72... | collective-permute-start | bytes 786440 | tf_op jit(solution)/shard_map/ppermute | solution.py:203

commit v4 on v3

--- a/solution.py
+++ b/solution.py
@@ -22,24 +22,60 @@
     return (at + 1 - 2 * (at % 2)) % 4 if not odd else (at - 1 + 2 * (at % 2)) % 4
 
 
-def landings(block, replica):
-    z, x, core = block // 8, block // 2 % 4, block % 2
-    owner = block // 4
-    away = (replica % 4 - owner % 4) % 4
-    beside = (x + 1 if x % 2 else x - 1) % 4
-    near = [z, partner(z, core)]
-    if replica // 4 != owner // 4:
-        near = [p for p in range(4) if p not in near]
-    if away % 3 == 0:
-        x = beside
-    if away % 2:
-        near.reverse()
-    if away == 3:
-        near.reverse()
-    if away == 0:
-        near.reverse()
-    planes = near + [partner(p, 1 - core) for p in near]
-    return [section_of(p, x, core) for p in planes], owner
+def cheapest(cost):
+    n = len(cost)
+    rows, columns = [0] * (n + 1), [0] * (n + 1)
+    owner, back = [0] * (n + 1), [0] * (n + 1)
+    for row in range(1, n + 1):
+        owner[0], at = row, 0
+        least, used = [float("inf")] * (n + 1), [False] * (n + 1)
+        while True:
+            used[at] = True
+            here = owner[at]
+            for j in range(1, n + 1):
+                over = cost[here - 1][j - 1] - rows[here] - columns[j]
+                if not used[j] and over < least[j]:
+                    least[j], back[j] = over, at
+            nearest = min((j for j in range(1, n + 1) if not used[j]), key=lambda j: least[j])
+            step = least[nearest]
+            for j in range(n + 1):
+                if used[j]:
+                    rows[owner[j]] += step
+                    columns[j] -= step
+                else:
+                    least[j] -= step
+            at = nearest
+            if owner[at] == 0:
+                break
+        while at:
+            owner[at] = owner[back[at]]
+            at = back[at]
+    return [owner.index(row, 1) - 1 for row in range(1, n + 1)]
+
+
+def landings():
+    lands = [[], [], [], []]
+    spots = [(z, x) for z in range(4) for x in range(4)]
+    for owner in range(REPS):
+        for core in range(2):
+            blocks = range(4 * owner + core, 4 * owner + 4, 2)
+            chunks = [(block, replica) for block in blocks for replica in range(REPS)]
+            been = [set() for _ in chunks]
+            for pairs in lands:
+                cost = []
+                for (block, replica), planes in zip(chunks, been):
+                    beyond = [
+                        abs((2 * z + owner // 4 - (block // 8 * 2 + replica // 4) + 4) % 8 - 4)
+                        + abs((owner % 4 - replica % 4 + 2) % 4 - 2)
+                        + abs((x - block // 2 % 4 + 2) % 4 - 2)
+                        for z, x in spots
+                    ]
+                    cost.append([10**7 if z in planes else hops**8 for (z, _), hops in zip(spots, beyond)])
+                for (block, replica), planes, spot in zip(chunks, been, cheapest(cost)):
+                    z, x = spots[spot]
+                    planes.add(z)
+                    pairs.append((block * REPS + replica, section_of(z, x, core) * REPS + owner))
+    return lands
 
 
 def swaps(step):
@@ -50,12 +86,7 @@
     return pairs
 
 
-LANDS = [[], [], [], []]
-for _b in range(SECTIONS):
-    for _r in range(REPS):
-        _places, _o = landings(_b, _r)
-        for _pairs, _s in zip(LANDS, _places):
-            _pairs.append((_b * REPS + _r, _s * REPS + _o))
+LANDS = landings()
 CORES = [(s, s ^ 1) for s in range(SECTIONS)]
 X_SWAPS = [swaps(0), swaps(1)]
 

time: 58.1 us -> 56.8 us (0.978)
  starting transfers between devices: 29 us -> 24 us
  waiting for transfers between devices: 1.25 us -> 3.11 us
  Pallas kernels: 10.9 us -> 12.2 us
    ppermute x4, starting transfers between devices: 18.1 us -> 13.8 us  [body(): lax.ppermute(features, ('section', 'rep'), pairs)]
    ppermute x4, waiting for transfers between devices: 0.01 us -> 2.32 us  [body(): lax.ppermute(features, ('section', 'rep'), pairs)]
    pallas_call x3, Pallas kernels: 4.1 us -> 4.89 us  [add_stage(): pl.pallas_call(functools.partial(stage_kernel, stage), out_shape=jax.Shap...]
    ppermute x7, starting transfers between devices: 10.8 us -> 10.2 us  [swap(): return lax.ppermute(array, 'section', pairs)]
  transfers between devices with their start and end apart: 11 -> 11, of which waited for: 1 -> 2; matrix products, arithmetic and copies ran while one was open for 2% -> 2% of each run, Pallas kernels for 15% -> 18%
where the time goes in v4:
time: 56.8 us; the launch traced here: 56.4 us
  starting transfers between devices  24 us (42%)
  blocking collectives  15.4 us (27%)
  Pallas kernels  12.2 us (21%)
  waiting for transfers between devices  3.11 us (5%)
  other arithmetic  0.73 us (1%)
  local copies, waits for them, and re-layouts  0.69 us (1%)
    all_to_all x1, blocking collectives, body(): parts = lax.all_to_all(partial_sums, 'rep', 0, 0, tiled=True)  15.4 us
    ppermute x4, starting transfers between devices, body(): lax.ppermute(features, ('section', 'rep'), pairs)  13.8 us
    ppermute x7, starting transfers between devices, swap(): return lax.ppermute(array, 'section', pairs)  10.2 us
    pallas_call x3, Pallas kernels, add_stage(): pl.pallas_call(functools.partial(stage_kernel, stage), out_shape=jax.Shap...  4.89 us
    pallas_call x1, Pallas kernels, body(): pl.pallas_call(load_kernel, out_shape=jax.ShapeDtypeStruct(vals.shape, va...  3.33 us
    pallas_call x1, Pallas kernels, body(): pl.pallas_call(list_kernel, out_shape=jax.ShapeDtypeStruct((len(STAGES) *...  3.14 us
    ppermute x4, waiting for transfers between devices, body(): lax.ppermute(features, ('section', 'rep'), pairs)  2.32 us
  transfers between devices with their start and end apart: 11, of which 2 were waited for; matrix products, arithmetic and copies ran while one was open for 2% of the time, Pallas kernels for 18%

profile of v4, /device:TPU:1, one launch (start us, length us, event | category | flops | bytes accessed | tf_op | source)
XLA Modules:
  0.0 56.4 jit_solution(2371871009477328483)
XLA Ops:
  0.0 9.9 %collective-permute-start.1 = (bf16[256,128]{1,0:T(8,128)(2,1)}, bf16[256,128]{1,0:T(8,128)(2,1)S(1)}, u32[]{:S(2)}, u32[]{:S(2)}) collective-permute-start(bf16[256,128]{1,0:T(8,128)(2,1)} %param.7), channel_id=1, source_target_pairs={{0,176},{1,240},{2,192},{3,48},{4,112},{5,128},{6,0},{7,64},{16,16... | collective-permute-start | bytes 196616 | tf_op jit(solution)/shard_map/ppermute | solution.py:244
  9.9 2.3 %collective-permute-start = (bf16[256,128]{1,0:T(8,128)(2,1)}, bf16[256,128]{1,0:T(8,128)(2,1)S(1)}, u32[]{:S(2)}, u32[]{:S(2)}) collective-permute-start(bf16[256,128]{1,0:T(8,128)(2,1)} %param.7), channel_id=1, source_target_pairs={{0,240},{1,48},{2,0},{3,192},{4,176},{5,112},{6,64},{7,128},{16,22... | collective-permute-start | bytes 196616 | tf_op jit(solution)/shard_map/ppermute | solution.py:244
  12.2 0.0 collective-permute-start.3
  12.2 1.6 %collective-permute-start.2 = (bf16[256,128]{1,0:T(8,128)(2,1)}, bf16[256,128]{1,0:T(8,128)(2,1)S(1)}, u32[]{:S(2)}, u32[]{:S(2)}) collective-permute-start(bf16[256,128]{1,0:T(8,128)(2,1)} %param.7), channel_id=1, source_target_pairs={{0,48},{1,128},{2,64},{3,112},{4,240},{5,0},{6,176},{7,192},{16,32... | collective-permute-start | bytes 196616 | tf_op jit(solution)/shard_map/ppermute | solution.py:244
  13.8 0.7 %constant_dynamic-slice_fusion = s32[1,4,16]{2,1,0:T(4,128)S(1)} fusion(s32[256,4,16]{2,1,0:T(4,128)} %constant.17.clone, s32[]{:T(128)S(6)} %select_n.3), kind=kLoop, calls=%fused_computation.2 | loop fusion | bytes 516 | tf_op jit(solution)/shard_map/dynamic_slice | solution.py:238
  14.5 0.7 %pad_add_fusion.small = s32[8,4,16]{2,1,0:T(4,128)S(1)} fusion(s32[6,4,16]{2,1,0:T(4,128)} %bitcast.9, s32[1,4,16]{2,1,0:T(4,128)} %param.12, s32[1,4,16]{2,1,0:T(4,128)S(1)} %constant_dynamic-slice_fusion), kind=kLoop, calls=%fused_computation.1 | loop fusion | flops 1024 | bytes 4096 | tf_op jit(solution)/shard_map/concatenate | solution.py:236
  15.2 3.1 %list_live_tiles.1.entries = s32[1179]{0:T(1024)S(1)} custom-call(s32[8,4,16]{2,1,0:T(4,128)S(1)} %pad_add_fusion.small), custom_call_target="tpu_custom_call" | custom-call | flops 4000 | bytes 4096 | tf_op jit(solution)/shard_map/list_live_tiles/pallas_call | solution.py:245
  18.3 0.0 collective-permute-done.1
  18.3 0.0 collective-permute-done
  18.3 0.0 collective-permute-done.3
  18.4 2.3 %collective-permute-done.2 = bf16[256,128]{1,0:T(8,128)(2,1)S(1)} collective-permute-done((bf16[256,128]{1,0:T(8,128)(2,1)}, bf16[256,128]{1,0:T(8,128)(2,1)S(1)}, u32[]{:S(2)}, u32[]{:S(2)}) %collective-permute-start.2) | collective-permute-done | bytes 65568 | tf_op jit(solution)/shard_map/ppermute | solution.py:244
  20.7 0.1 collective-permute-start.4
  20.8 0.1 collective-permute-start.6
  20.9 2.2 %collective-permute-start.7 = (bf16[1024,128]{1,0:T(8,128)(2,1)S(1)}, bf16[1024,128]{1,0:T(8,128)(2,1)S(1)}, u32[]{:S(2)}, u32[]{:S(2)}) collective-permute-start(bf16[1024,128]{1,0:T(8,128)(2,1)S(1)} %pad_maximum_fusion.refs_0_), channel_id=1, source_target_pairs={{0,8},{8,0},{16,24},{24,16},{32,40},{40,32},{48,56},{56,48},{64,72... | collective-permute-start | bytes 786440 | tf_op jit(solution)/shard_map/ppermute | solution.py:234
  23.1 3.3 %load_live_tiles.1.vals = bf16[384,128,128]{2,1,0:T(8,128)(2,1)S(1)} custom-call(s32[8,4,16]{2,1,0:T(4,128)S(1)} %pad_add_fusion.small, bf16[384,128,128]{2,1,0:T(8,128)(2,1)} %bitcast.8), custom_call_target="tpu_custom_call" | custom-call | flops 4000 | bytes 25165824 | tf_op jit(solution)/shard_map/load_live_tiles/pallas_call | solution.py:261
  26.4 0.8 %collective-permute-done.4.refs_1_ = bf16[1024,128]{1,0:T(8,128)(2,1)S(1)} collective-permute-done((bf16[1024,128]{1,0:T(8,128)(2,1)S(1)}, bf16[1024,128]{1,0:T(8,128)(2,1)S(1)}, u32[]{:S(2)}, u32[]{:S(2)}) %collective-permute-start.4) | collective-permute-done | bytes 262176 | tf_op jit(solution)/shard_map/ppermute | solution.py:234
  27.2 0.6 %collective-permute-start.5 = (bf16[1024,128]{1,0:T(8,128)(2,1)S(1)}, bf16[1024,128]{1,0:T(8,128)(2,1)S(1)}, u32[]{:S(2)}, u32[]{:S(2)}) collective-permute-start(bf16[1024,128]{1,0:T(8,128)(2,1)S(1)} %collective-permute-done.4.refs_1_), channel_id=1, source_target_pairs={{0,48},{8,24},{16,32},{24,8},{32,16},{40,56},{48,0},{56,40},{64,11... | collective-permute-start | bytes 786440 | tf_op jit(solution)/shard_map/ppermute | solution.py:234
  27.8 1.8 %collective-permute-start.9 = (bf16[1024,128]{1,0:T(8,128)(2,1)S(1)}, bf16[1024,128]{1,0:T(8,128)(2,1)S(1)}, u32[]{:S(2)}, u32[]{:S(2)}) collective-permute-start(bf16[1024,128]{1,0:T(8,128)(2,1)S(1)} %collective-permute-done.4.refs_1_), channel_id=1, source_target_pairs={{0,8},{8,0},{16,24},{24,16},{32,40},{40,32},{48,56},{56,48},{64,72... | collective-permute-start | bytes 786440 | tf_op jit(solution)/shard_map/ppermute | solution.py:234
  29.6 0.0 collective-permute-done.6.refs_2_
  29.6 1.1 %collective-permute-start.10 = (bf16[1024,128]{1,0:T(8,128)(2,1)S(1)}, bf16[1024,128]{1,0:T(8,128)(2,1)S(1)}, u32[]{:S(2)}, u32[]{:S(2)}) collective-permute-start(bf16[1024,128]{1,0:T(8,128)(2,1)S(1)} %collective-permute-done.6.refs_2_), channel_id=1, source_target_pairs={{0,8},{8,0},{16,24},{24,16},{32,40},{40,32},{48,56},{56,48},{64,72... | collective-permute-start | bytes 786440 | tf_op jit(solution)/shard_map/ppermute | solution.py:234
  30.7 0.0 collective-permute-done.7.refs_3_
  30.7 2.1 %sum_stage_0.1.refs_0_ = f32[2048,128]{1,0:T(8,128)S(1)} custom-call(s32[1179]{0:T(1024)S(1)} %list_live_tiles.1.entries, bf16[384,128,128]{2,1,0:T(8,128)(2,1)S(1)} %load_live_tiles.1.vals, bf16[1024,128]{1,0:T(8,128)(2,1)S(1)} %pad_maximum_fusion.refs_0_, bf16[1024,128]{1,0:T(8,128)(2,1)S(1)} %collective-permute-done.4.refs_1_, ...), custom_call_target="tpu_custom_call" | custom-call | flops 22364160 | bytes 1048576 | tf_op jit(solution)/shard_map/sum_stage_0/pallas_call | solution.py:281
  32.8 0.0 copy-start
  32.8 0.0 copy-start.1
  32.8 0.0 collective-permute-done.5.refs_1_
  32.8 4.4 %collective-permute-start.8 = (bf16[1024,128]{1,0:T(8,128)(2,1)S(1)}, bf16[1024,128]{1,0:T(8,128)(2,1)S(1)}, u32[]{:S(2)}, u32[]{:S(2)}) collective-permute-start(bf16[1024,128]{1,0:T(8,128)(2,1)S(1)} %collective-permute-done.5.refs_1_), channel_id=1, source_target_pairs={{0,8},{8,0},{16,24},{24,16},{32,40},{40,32},{48,56},{56,48},{64,72... | collective-permute-start | bytes 786440 | tf_op jit(solution)/shard_map/ppermute | solution.py:234
  37.2 0.0 collective-permute-done.10.refs_3_
  37.2 0.0 collective-permute-done.9.refs_2_
  37.2 1.8 %sum_stage_1.1.refs_0_ = f32[2048,128]{1,0:T(8,128)S(1)} custom-call(s32[1179]{0:T(1024)S(1)} %list_live_tiles.1.entries, bf16[384,128,128]{2,1,0:T(8,128)(2,1)S(1)} %load_live_tiles.1.vals, f32[2048,128]{1,0:T(8,128)S(1)} %sum_stage_0.1.refs_0_, bf16[1024,128]{1,0:T(8,128)(2,1)S(1)} %collective-permute-done.5.refs_1_, ...), custom_call_target="tpu_custom_call" | custom-call | flops 16777216 | bytes 1048576 | tf_op jit(solution)/shard_map/sum_stage_1/pallas_call | solution.py:281
  39.0 0.0 collective-permute-done.8.refs_1_
  39.0 1.0 %sum_stage_2.1 = bf16[2048,128]{1,0:T(8,128)(2,1)S(1)} custom-call(s32[1179]{0:T(1024)S(1)} %list_live_tiles.1.entries, bf16[384,128,128]{2,1,0:T(8,128)(2,1)S(1)} %load_live_tiles.1.vals, f32[2048,128]{1,0:T(8,128)S(1)} %sum_stage_1.1.refs_0_, bf16[1024,128]{1,0:T(8,128)(2,1)S(1)} %collective-permute-done.8.refs_1_), custom_call_target="tpu_custom_call" | custom-call | flops 5586944 | bytes 1048576 | tf_op jit(solution)/shard_map/sum_stage_2/pallas_call | solution.py:281
  40.0 15.4 %all_to_all.9.parts = bf16[8,256,128]{2,1,0:T(8,128)(2,1)S(1)} all-to-all(bf16[8,256,128]{2,1,0:T(8,128)(2,1)S(1)} %bitcast.6), channel_id=1, replica_groups=mesh['section'=32,'rep'=8] {'rep'}, dimensions={0} | all-to-all | bytes 1048576 | tf_op jit(solution)/shard_map/all_to_all | solution.py:299
  55.5 0.0 copy-done
  55.5 0.0 copy-done.1
  55.5 0.9 %apply_weight.1 = bf16[256,256]{1,0:T(8,128)(2,1)} custom-call(bf16[8,256,128]{2,1,0:T(8,128)(2,1)S(1)} %all_to_all.9.parts, bf16[128,256]{1,0:T(8,128)(2,1)S(1)} %copy-done, f32[1,256]{1,0:T(1,128)S(1)} %bitcast.7), custom_call_target="tpu_custom_call" | custom-call | flops 33554432 | bytes 1048576 | tf_op jit(solution)/shard_map/apply_weight/pallas_call | solution.py:300
  (1 shorter events, 0.0 us)
Async XLA Ops:
  0.0 18.3 %collective-permute-start.1 = (bf16[256,128]{1,0:T(8,128)(2,1)}, bf16[256,128]{1,0:T(8,128)(2,1)S(1)}, u32[]{:S(2)}, u32[]{:S(2)}) collective-permute-start(bf16[256,128]{1,0:T(8,128)(2,1)} %param.7), channel_id=1, source_target_pairs={{0,176},{1,240},{2,192},{3,48},{4,112},{5,128},{6,0},{7,64},{16,16... | collective-permute-start | bytes 196616 | tf_op jit(solution)/shard_map/ppermute | solution.py:244
  9.9 8.4 %collective-permute-start = (bf16[256,128]{1,0:T(8,128)(2,1)}, bf16[256,128]{1,0:T(8,128)(2,1)S(1)}, u32[]{:S(2)}, u32[]{:S(2)}) collective-permute-start(bf16[256,128]{1,0:T(8,128)(2,1)} %param.7), channel_id=1, source_target_pairs={{0,240},{1,48},{2,0},{3,192},{4,176},{5,112},{6,64},{7,128},{16,22... | collective-permute-start | bytes 196616 | tf_op jit(solution)/shard_map/ppermute | solution.py:244
  12.2 6.1 %collective-permute-start.3 = (bf16[256,128]{1,0:T(8,128)(2,1)}, bf16[256,128]{1,0:T(8,128)(2,1)S(1)}, u32[]{:S(2)}, u32[]{:S(2)}) collective-permute-start(bf16[256,128]{1,0:T(8,128)(2,1)} %param.7), channel_id=1, source_target_pairs={{0,112},{1,64},{2,128},{3,176},{4,48},{5,240},{6,192},{7,0},{16,96... | collective-permute-start | bytes 196616 | tf_op jit(solution)/shard_map/ppermute | solution.py:244
  12.2 8.4 %collective-permute-start.2 = (bf16[256,128]{1,0:T(8,128)(2,1)}, bf16[256,128]{1,0:T(8,128)(2,1)S(1)}, u32[]{:S(2)}, u32[]{:S(2)}) collective-permute-start(bf16[256,128]{1,0:T(8,128)(2,1)} %param.7), channel_id=1, source_target_pairs={{0,48},{1,128},{2,64},{3,112},{4,240},{5,0},{6,176},{7,192},{16,32... | collective-permute-start | bytes 196616 | tf_op jit(solution)/shard_map/ppermute | solution.py:244
  20.7 6.5 %collective-permute-start.4 = (bf16[1024,128]{1,0:T(8,128)(2,1)S(1)}, bf16[1024,128]{1,0:T(8,128)(2,1)S(1)}, u32[]{:S(2)}, u32[]{:S(2)}) collective-permute-start(bf16[1024,128]{1,0:T(8,128)(2,1)S(1)} %pad_maximum_fusion.refs_0_), channel_id=1, source_target_pairs={{0,16},{8,56},{16,0},{24,40},{32,48},{40,24},{48,32},{56,8},{64,80... | collective-permute-start | bytes 786440 | tf_op jit(solution)/shard_map/ppermute | solution.py:234
  20.8 8.8 %collective-permute-start.6 = (bf16[1024,128]{1,0:T(8,128)(2,1)S(1)}, bf16[1024,128]{1,0:T(8,128)(2,1)S(1)}, u32[]{:S(2)}, u32[]{:S(2)}) collective-permute-start(bf16[1024,128]{1,0:T(8,128)(2,1)S(1)} %pad_maximum_fusion.refs_0_), channel_id=1, source_target_pairs={{0,48},{8,24},{16,32},{24,8},{32,16},{40,56},{48,0},{56,40},{64,11... | collective-permute-start | bytes 786440 | tf_op jit(solution)/shard_map/ppermute | solution.py:234
  20.9 9.8 %collective-permute-start.7 = (bf16[1024,128]{1,0:T(8,128)(2,1)S(1)}, bf16[1024,128]{1,0:T(8,128)(2,1)S(1)}, u32[]{:S(2)}, u32[]{:S(2)}) collective-permute-start(bf16[1024,128]{1,0:T(8,128)(2,1)S(1)} %pad_maximum_fusion.refs_0_), channel_id=1, source_target_pairs={{0,8},{8,0},{16,24},{24,16},{32,40},{40,32},{48,56},{56,48},{64,72... | collective-permute-start | bytes 786440 | tf_op jit(solution)/shard_map/ppermute | solution.py:234
  27.2 5.6 %collective-permute-start.5 = (bf16[1024,128]{1,0:T(8,128)(2,1)S(1)}, bf16[1024,128]{1,0:T(8,128)(2,1)S(1)}, u32[]{:S(2)}, u32[]{:S(2)}) collective-permute-start(bf16[1024,128]{1,0:T(8,128)(2,1)S(1)} %collective-permute-done.4.refs_1_), channel_id=1, source_target_pairs={{0,48},{8,24},{16,32},{24,8},{32,16},{40,56},{48,0},{56,40},{64,11... | collective-permute-start | bytes 786440 | tf_op jit(solution)/shard_map/ppermute | solution.py:234
  27.8 9.4 %collective-permute-start.9 = (bf16[1024,128]{1,0:T(8,128)(2,1)S(1)}, bf16[1024,128]{1,0:T(8,128)(2,1)S(1)}, u32[]{:S(2)}, u32[]{:S(2)}) collective-permute-start(bf16[1024,128]{1,0:T(8,128)(2,1)S(1)} %collective-permute-done.4.refs_1_), channel_id=1, source_target_pairs={{0,8},{8,0},{16,24},{24,16},{32,40},{40,32},{48,56},{56,48},{64,72... | collective-permute-start | bytes 786440 | tf_op jit(solution)/shard_map/ppermute | solution.py:234
  29.6 7.6 %collective-permute-start.10 = (bf16[1024,128]{1,0:T(8,128)(2,1)S(1)}, bf16[1024,128]{1,0:T(8,128)(2,1)S(1)}, u32[]{:S(2)}, u32[]{:S(2)}) collective-permute-start(bf16[1024,128]{1,0:T(8,128)(2,1)S(1)} %collective-permute-done.6.refs_2_), channel_id=1, source_target_pairs={{0,8},{8,0},{16,24},{24,16},{32,40},{40,32},{48,56},{56,48},{64,72... | collective-permute-start | bytes 786440 | tf_op jit(solution)/shard_map/ppermute | solution.py:234
  32.8 22.7 %copy-start = (bf16[128,256]{1,0:T(8,128)(2,1)S(1)}, bf16[128,256]{1,0:T(8,128)(2,1)}, u32[]{:S(2)}) copy-start(bf16[128,256]{1,0:T(8,128)(2,1)} %weight.1) | copy-start | bytes 196612
  32.8 22.7 %copy-start.1 = (f32[256]{0:T(256)S(1)}, f32[256]{0:T(256)}, u32[]{:S(2)}) copy-start(f32[256]{0:T(256)} %param.9) | copy-start | bytes 3076
  32.8 6.2 %collective-permute-start.8 = (bf16[1024,128]{1,0:T(8,128)(2,1)S(1)}, bf16[1024,128]{1,0:T(8,128)(2,1)S(1)}, u32[]{:S(2)}, u32[]{:S(2)}) collective-permute-start(bf16[1024,128]{1,0:T(8,128)(2,1)S(1)} %collective-permute-done.5.refs_1_), channel_id=1, source_target_pairs={{0,8},{8,0},{16,24},{24,16},{32,40},{40,32},{48,56},{56,48},{64,72... | collective-permute-start | bytes 786440 | tf_op jit(solution)/shard_map/ppermute | solution.py:234
